TPU v7x, 128 devices: a whole 4x4x4 slice. The times are simulated.
128 devices in a mesh: dp: 128 (over x, y, z, core).
Axes of the slice: x: 4, y: 4, z: 4, core: 2. Of those that a mesh axis runs over, the one named last changes fastest.
Arguments:
- tokens: bfloat16 [256, 512, 576], P('dp'), may hold values from -6 to 6
- positions: int32 [256, 512], P('dp'), may hold values from 0 to 8191, as said below
- norm_gains: bfloat16 [1152], P('dp'), may hold values from 0.25 to 1.75
- w_query: bfloat16 [331776], P('dp'), may hold values from -0.25 to 0.25
- w_key: bfloat16 [110592], P('dp'), may hold values from -0.25 to 0.25
- w_value: bfloat16 [110592], P('dp'), may hold values from -0.25 to 0.25
- w_out: bfloat16 [331776], P('dp'), may hold values from -1 to 1
- w_gate: bfloat16 [884736], P('dp'), may hold values from -0.25 to 0.25
- w_up: bfloat16 [884736], P('dp'), may hold values from -0.25 to 0.25
- w_down: bfloat16 [884736], P('dp'), may hold values from -0.3125 to 0.3125
- cotangent: float32 [256, 512, 576], P('dp')
Outputs:
- output: bfloat16 [256, 512, 576], P('dp')
- grad_tokens: float32 [256, 512, 576], P('dp')
- grad_gains: float32 [1152], P('dp')
- grad_query: float32 [331776], P('dp')
- grad_key: float32 [110592], P('dp')
- grad_value: float32 [110592], P('dp')
- grad_out: float32 [331776], P('dp')
- grad_gate: float32 [884736], P('dp')
- grad_up: float32 [884736], P('dp')
- grad_down: float32 [884736], P('dp')
Inputs may be any that keep to these rules, and one draw needn't show every extreme that they name: Each row is a run of packed documents: positions count up by one within a document, and every document after a row's first starts at 0; in every draw one row starts at 0, and one row is a single document that ends at 8191.
All inputs are finite; a program needn't handle non-finite values.
Results may differ from a plain program's by a relative error of at most 0.015.
Values may be sent and summed in bfloat16 or wider, within the bound.
No kernel may reach another device: no remote copies, remote signals or barrier semaphores. Data moves between devices by JAX's collectives and lax.ppermute only.
A program may use at most 192 MiB of HBM per device.

v0:
```python
import functools

import jax
import jax.numpy as jnp
from jax import lax
from jax.sharding import PartitionSpec as P
from jax.experimental import pallas as pl
from jax.experimental.pallas import tpu as pltpu

D = 576
HEADS = 9
KV_HEADS = 3
HEAD = 64
FF = 1536
SEQ = 512
KVW = KV_HEADS * HEAD
QKV = D + 2 * KVW
HALF = SEQ // 2

EPSILON = 1e-05
NEG_FILL = -1e30

F32 = jnp.float32
BF16 = jnp.bfloat16

CHIPS = 64
R_GATE = 54
R_DOWN = 60
R_OUT = 27
R_KEY = 9
F_GATE, F_UP, F_DOWN, F_OUT, ROWS_F = 0, 54, 112, 172, 208
B_GATE, B_UP, ROWS_B = 0, 54, 112
G_DOWN, G_OUT, ROWS_G = 0, 60, 96
Q_QUERY, Q_KEY, Q_VALUE, Q_GAIN, ROWS_Q = 0, 27, 36, 45, 48

NN = (((1,), (0,)), ((), ()))
NT = (((1,), (1,)), ((), ()))
TN = (((0,), (0,)), ((), ()))


def mm(a, b, dims=NN):
    return lax.dot_general(a, b, dims, preferred_element_type=F32)


def whole_spec(shape):
    zeros = (0,) * len(shape)
    return pl.BlockSpec(shape, lambda i: zeros)


def seq_spec(shape, at=None):
    zeros = (0,) * len(shape)
    return pl.BlockSpec((1,) + shape, lambda i: (i if at is None else at,) + zeros)


def chip_of(slot, where_ref, swap):
    one, two, three = slot // 16, (slot // 4) % 4, slot % 4
    kz, ky = (two, one) if swap else (one, two)
    x = (where_ref[1] + three) % 4
    y = (where_ref[2] + ky) % 4
    z = (where_ref[3] + kz) % 4
    return (x * 4 + y) * 4 + z


def put_rows(ref, dev, rows, val):
    ref[pl.ds(dev * rows, rows), :] = val


def get_rows(ref, dev, rows):
    return ref[pl.ds(dev * rows, rows), :]


def split_square(ref):
    parts = []
    for half in range(2):
        for j in range(3):
            piece = ref[pl.ds(3 * half + j, D, stride=6), :]
            parts.append(piece if j < 2 else piece[:, :32])
    return parts


def join_square(ref, val_ref):
    for half in range(2):
        for j in range(3):
            width = 128 if j < 2 else 32
            at = 288 * half + 128 * j
            ref[pl.ds(3 * half + j, D, stride=6), :width] = val_ref[:, at : at + width]


def pack_kernel(wqo, wkv, gn, wd, wgu, f_ref, q_ref, f_stage_ref, q_stage_ref):
    f_stage_ref[...] = jnp.zeros_like(f_stage_ref)
    q_stage_ref[...] = jnp.zeros_like(q_stage_ref)
    square = wqo[...].astype(F32)
    thin = wkv[...].astype(F32)
    for ref, at, val in (
        (q_stage_ref, Q_QUERY, square[:R_OUT]),
        (q_stage_ref, Q_KEY, thin[:R_KEY]),
        (q_stage_ref, Q_VALUE, thin[R_KEY:]),
        (q_stage_ref, Q_GAIN, gn[...].astype(F32)),
        (f_stage_ref, F_GATE, wgu[...].astype(F32)),
        (f_stage_ref, F_DOWN, wd[...].astype(F32)),
        (f_stage_ref, F_OUT, square[R_OUT:]),
    ):
        ref[at : at + val.shape[0], : val.shape[1]] = val
    f_ref[...] = f_stage_ref[...].astype(BF16)
    q_ref[...] = q_stage_ref[...].astype(BF16)


def pack(pieces):
    vmem = pl.BlockSpec(memory_space=pltpu.VMEM)
    return pl.pallas_call(
        pack_kernel,
        in_specs=[vmem] * 5,
        out_specs=[vmem] * 2,
        out_shape=[
            jax.ShapeDtypeStruct((ROWS_F, 128), BF16),
            jax.ShapeDtypeStruct((ROWS_Q, 128), BF16),
        ],
        scratch_shapes=[pltpu.VMEM((ROWS_F, 128), F32), pltpu.VMEM((ROWS_Q, 128), F32)],
        name="pack",
    )(*pieces)


def lane_rows(v, rows, width):
    v = v.reshape(rows, width)
    full = -(-width // 128) * 128
    v = jnp.pad(v, ((0, 0), (0, full - width)))
    return v.reshape(rows * full // 128, 128)


def take_lanes(v, rows, width):
    full = -(-width // 128) * 128
    return v.reshape(rows, full)[:, :width].reshape(-1)


def rope_rows(v, cos_t, sin_t, heads, sign):
    out = []
    for head in range(heads):
        lo = v[head * HEAD : head * HEAD + 32]
        hi = v[head * HEAD + 32 : head * HEAD + 64]
        if sign > 0:
            out += [lo * cos_t - hi * sin_t, hi * cos_t + lo * sin_t]
        else:
            out += [lo * cos_t + hi * sin_t, hi * cos_t - lo * sin_t]
    return jnp.concatenate(out, axis=0)


def attn_fwd_kernel(
    pack_ref, x_ref, cos_ref, sin_ref, docr_ref, docc_ref,
    wqkv_ref, gain_ref, h_t_ref, q_t_ref, k_t_ref, v_t_ref, p_ref, o_t_ref,
    qs_ref, ks_ref, vs_ref, gs_ref, w_t_ref, bias_ref, k_ref,
):
    @pl.when(pl.program_id(0) == 0)
    def _():
        def squeeze(dev, carry):
            val = pack_ref[dev].astype(F32)
            put_rows(qs_ref, dev, R_OUT, val[Q_QUERY : Q_QUERY + R_OUT])
            put_rows(ks_ref, dev, R_KEY, val[Q_KEY : Q_KEY + R_KEY])
            put_rows(vs_ref, dev, R_KEY, val[Q_VALUE : Q_VALUE + R_KEY])
            put_rows(gs_ref, dev, 1, val[Q_GAIN : Q_GAIN + 1])
            return carry

        lax.fori_loop(0, 2 * CHIPS, squeeze, 0)
        parts = split_square(qs_ref)
        for ref in (ks_ref, vs_ref):
            for half in range(2):
                parts.append(ref[pl.ds(half, D, stride=2), :][:, :96])
        whole = jnp.concatenate(parts, axis=1)
        wqkv_ref[...] = whole.astype(BF16)
        w_t_ref[...] = whole.T.astype(BF16)
        for lane in range(9):
            gain_ref[pl.ds(lane, 2 * CHIPS, stride=9), :] = gs_ref[:, lane : lane + 1]

    x = x_ref[0].astype(F32)
    inv = lax.rsqrt(jnp.mean(x * x, axis=0, keepdims=True) + EPSILON)
    h_t = ((x * inv) * gain_ref[:D]).astype(BF16)
    h_t_ref[0] = h_t
    cos_t = cos_ref[0]
    sin_t = sin_ref[0]
    q_t = mm(w_t_ref[:D], h_t)
    q_t_ref[0] = rope_rows(q_t, cos_t, sin_t, HEADS, 1).astype(BF16) * 0.125
    k_t = rope_rows(mm(w_t_ref[D : D + KVW], h_t), cos_t, sin_t, KV_HEADS, 1).astype(BF16)
    k_t_ref[0] = k_t
    for group in range(KV_HEADS):
        k_ref[group] = k_t[group * HEAD : (group + 1) * HEAD].astype(F32).T.astype(BF16)
    v_t_ref[0] = mm(w_t_ref[D + KVW :], h_t).astype(BF16)
    key_at = lax.broadcasted_iota(jnp.int32, (SEQ, SEQ), 0)
    query_at = lax.broadcasted_iota(jnp.int32, (SEQ, SEQ), 1)
    same = docc_ref[0] == docr_ref[0]
    bias_ref[...] = jnp.where(same & (key_at <= query_at), 0.0, NEG_FILL)

    def group_step(group, carry):
        kv_rows = pl.ds(pl.multiple_of(group * HEAD, HEAD), HEAD)
        for member in range(HEADS // KV_HEADS):
            head = group * (HEADS // KV_HEADS) + member
            rows = pl.ds(pl.multiple_of(head * HEAD, HEAD), HEAD)
            for block in range(2):
                cols = slice(block * HALF, (block + 1) * HALF)
                keys = slice(0, (block + 1) * HALF)
                s_t = mm(k_ref[group, keys, :], q_t_ref[0, rows, cols]) + bias_ref[keys, cols]
                peak = jnp.max(s_t, axis=0, keepdims=True)
                e_t = jnp.exp(s_t - peak)
                scale = 1.0 / jnp.sum(e_t, axis=0, keepdims=True)
                p_t = (e_t * scale).astype(BF16)
                p_ref[0, head, keys, cols] = p_t
                o_t_ref[0, rows, cols] = mm(v_t_ref[0, kv_rows, keys], p_t).astype(BF16)
        return carry

    lax.fori_loop(0, KV_HEADS, group_step, 0)


def attn_fwd(pack_q, x_t, cos_t, sin_t, doc_row, doc_col):
    seqs = x_t.shape[0]
    out = [
        ((D, QKV), BF16, False),
        ((2 * D, 1), F32, False),
        ((D, SEQ), BF16, True),
        ((D, SEQ), BF16, True),
        ((KVW, SEQ), BF16, True),
        ((KVW, SEQ), BF16, True),
        ((HEADS, SEQ, SEQ), BF16, True),
        ((D, SEQ), BF16, True),
    ]
    return pl.pallas_call(
        attn_fwd_kernel,
        grid=(seqs,),
        in_specs=[
            whole_spec((2 * CHIPS, ROWS_Q, 128)),
            seq_spec((D, SEQ)),
            seq_spec((32, SEQ)),
            seq_spec((32, SEQ)),
            seq_spec((1, SEQ)),
            seq_spec((SEQ, 1)),
        ],
        out_specs=[seq_spec(s) if per else whole_spec(s) for s, _, per in out],
        out_shape=[jax.ShapeDtypeStruct(((seqs,) + s) if per else s, t) for s, t, per in out],
        scratch_shapes=[
            pltpu.VMEM((2 * CHIPS * R_OUT, 128), F32),
            pltpu.VMEM((2 * CHIPS * R_KEY, 128), F32),
            pltpu.VMEM((2 * CHIPS * R_KEY, 128), F32),
            pltpu.VMEM((2 * CHIPS, 128), F32),
            pltpu.VMEM((QKV, D), BF16),
            pltpu.VMEM((SEQ, SEQ), F32),
            pltpu.VMEM((KV_HEADS, SEQ, HEAD), BF16),
        ],
        compiler_params=pltpu.CompilerParams(vmem_limit_bytes=63 * 2**20),
        cost_estimate=pl.CostEstimate(
            flops=8 * 10**9, bytes_accessed=20 * 10**6, transcendentals=5 * 10**6
        ),
        name="attn_fwd",
    )(pack_q, x_t, cos_t, sin_t, doc_row, doc_col)


CHUNK = 256
CHUNKS = FF // CHUNK


def ffn_kernel(
    where_ref, pack_ref, x_ref, o_t_ref, cot_ref, gain_ref,
    y_ref, dx1_ref, do_t_ref, dgain_ref, send_g_ref, keep_g_ref, send_b_ref, keep_b_ref,
    gs_ref, us_ref, ds_ref, os_ref, wg_ref, wu_ref, wd_ref, wo_ref,
    acc_ref, h_t_ref, gb_ref, dh_ref, inv_ref, stage_ref,
):
    seqs = x_ref.shape[0]
    core = where_ref[0]

    def squeeze(dev, carry):
        val = pack_ref[dev].astype(F32)
        put_rows(gs_ref, dev, R_GATE, val[F_GATE : F_GATE + R_GATE])
        put_rows(us_ref, dev, R_GATE, val[F_UP : F_UP + R_GATE])
        put_rows(ds_ref, dev, R_DOWN, val[F_DOWN : F_DOWN + R_DOWN])
        put_rows(os_ref, dev, R_OUT, val[F_OUT : F_OUT + R_OUT])
        return carry

    lax.fori_loop(0, 2 * CHIPS, squeeze, 0)
    wo_ref[...] = jnp.concatenate(split_square(os_ref), axis=1).astype(BF16)
    for j in range(12):
        cols = slice(j * 128, (j + 1) * 128)
        wg_ref[:, cols] = gs_ref[pl.ds(j, D, stride=12), :].astype(BF16)
        wu_ref[:, cols] = us_ref[pl.ds(j, D, stride=12), :].astype(BF16)
    for j in range(5):
        width = min(128, D - j * 128)
        wd_ref[:, j * 128 : j * 128 + width] = ds_ref[pl.ds(j, FF, stride=5), :][:, :width].astype(BF16)

    gain = gain_ref[D:]
    for seq in range(seqs):
        cols = slice(seq * SEQ, (seq + 1) * SEQ)
        x1 = x_ref[seq].astype(F32) + mm(wo_ref[...], o_t_ref[seq], TN)
        inv = lax.rsqrt(jnp.mean(x1 * x1, axis=0, keepdims=True) + EPSILON)
        normed = x1 * inv
        acc_ref[:, cols] = x1
        inv_ref[:, cols] = inv
        dx1_ref[seq] = normed
        h_t_ref[:, cols] = (normed * gain).astype(BF16)
        gb_ref[:, cols] = cot_ref[seq].astype(BF16)
    dh_ref[...] = jnp.zeros_like(dh_ref)

    def chunk_step(chunk, carry):
        cols = pl.ds(pl.multiple_of(chunk * CHUNK, CHUNK), CHUNK)
        wg = wg_ref[:, cols]
        wu = wu_ref[:, cols]
        wd = wd_ref[cols, :]
        h_t = h_t_ref[...]
        gb = gb_ref[...]
        a = mm(wg, h_t, TN)
        b = mm(wu, h_t, TN)
        dm = mm(wd, gb)
        sg = 1.0 / (1.0 + jnp.exp(-a))
        silu = a * sg
        m = (silu * b).astype(BF16)
        da = (dm * b * sg * (1.0 + a * (1.0 - sg))).astype(BF16)
        db = (dm * silu).astype(BF16)
        acc_ref[...] += mm(wd, m, TN)
        dh_ref[...] += mm(wg, da) + mm(wu, db)
        dwg = mm(h_t, da, NT)
        dwu = mm(h_t, db, NT)
        dwd = mm(m, gb, NT)
        for j in range(CHUNK // 128):
            lane = slice(j * 128, (j + 1) * 128)
            at = chunk * (CHUNK // 128) + j
            gs_ref[pl.ds(at, D, stride=12), :] = dwg[:, lane]
            us_ref[pl.ds(at, D, stride=12), :] = dwu[:, lane]
        for j in range(5):
            width = min(128, D - j * 128)
            ds_ref[pl.ds(chunk * CHUNK * 5 + j, CHUNK, stride=5), :width] = dwd[
                :, j * 128 : j * 128 + width
            ]
        return carry

    lax.fori_loop(0, CHUNKS, chunk_step, 0)

    dgain = jnp.zeros((D, 1), F32)
    dwo = jnp.zeros((D, D), F32)
    for seq in range(seqs):
        cols = slice(seq * SEQ, (seq + 1) * SEQ)
        y_ref[seq] = acc_ref[:, cols].astype(BF16)
        dh = dh_ref[:, cols]
        normed = dx1_ref[seq]
        dgain += jnp.sum(dh * normed, axis=1, keepdims=True)
        dn = dh * gain
        dx1 = cot_ref[seq] + inv_ref[:, cols] * (
            dn - normed * jnp.mean(dn * normed, axis=0, keepdims=True)
        )
        dx1_ref[seq] = dx1
        low = dx1.astype(BF16)
        dwo += mm(o_t_ref[seq], low, NT)
        do_t_ref[seq] = mm(wo_ref[...], low).astype(BF16)
    dgain_ref[...] = dgain
    dh_ref[:, :D] = dwo
    join_square(os_ref, dh_ref)

    stage_ref[...] = jnp.zeros_like(stage_ref)

    def spread(slot, carry):
        for keep_it in range(2):
            chip = chip_of(slot, where_ref, False)
            dev = chip * 2 + (core if keep_it else 1 - core)
            stage_ref[G_DOWN : G_DOWN + R_DOWN, :] = get_rows(ds_ref, dev, R_DOWN)
            stage_ref[G_OUT : G_OUT + R_OUT, :] = get_rows(os_ref, dev, R_OUT)
            (keep_g_ref if keep_it else send_g_ref)[slot] = stage_ref[:ROWS_G].astype(BF16)
            chip = chip_of(slot, where_ref, True)
            dev = chip * 2 + (core if keep_it else 1 - core)
            stage_ref[B_GATE : B_GATE + R_GATE, :] = get_rows(gs_ref, dev, R_GATE)
            stage_ref[B_UP : B_UP + R_GATE, :] = get_rows(us_ref, dev, R_GATE)
            (keep_b_ref if keep_it else send_b_ref)[slot] = stage_ref[...].astype(BF16)
        return carry

    lax.fori_loop(0, CHIPS, spread, 0)


def ffn(where, pack_f, x_t, o_t, cot_t, gain):
    seqs = x_t.shape[0]
    cols_all = seqs * SEQ
    vmem = pl.BlockSpec(memory_space=pltpu.VMEM)
    return pl.pallas_call(
        ffn_kernel,
        in_specs=[pl.BlockSpec(memory_space=pltpu.SMEM)] + [vmem] * 5,
        out_specs=[vmem] * 8,
        out_shape=[
            jax.ShapeDtypeStruct((seqs, D, SEQ), BF16),
            jax.ShapeDtypeStruct((seqs, D, SEQ), F32),
            jax.ShapeDtypeStruct((seqs, D, SEQ), BF16),
            jax.ShapeDtypeStruct((D, 1), F32),
            jax.ShapeDtypeStruct((CHIPS, ROWS_G, 128), BF16),
            jax.ShapeDtypeStruct((CHIPS, ROWS_G, 128), BF16),
            jax.ShapeDtypeStruct((CHIPS, ROWS_B, 128), BF16),
            jax.ShapeDtypeStruct((CHIPS, ROWS_B, 128), BF16),
        ],
        scratch_shapes=[
            pltpu.VMEM((2 * CHIPS * R_GATE, 128), F32),
            pltpu.VMEM((2 * CHIPS * R_GATE, 128), F32),
            pltpu.VMEM((2 * CHIPS * R_DOWN, 128), F32),
            pltpu.VMEM((2 * CHIPS * R_OUT, 128), F32),
            pltpu.VMEM((D, FF), BF16),
            pltpu.VMEM((D, FF), BF16),
            pltpu.VMEM((FF, D), BF16),
            pltpu.VMEM((D, D), BF16),
            pltpu.VMEM((D, cols_all), F32),
            pltpu.VMEM((D, cols_all), BF16),
            pltpu.VMEM((D, cols_all), BF16),
            pltpu.VMEM((D, cols_all), F32),
            pltpu.VMEM((1, cols_all), F32),
            pltpu.VMEM((ROWS_B, 128), F32),
        ],
        compiler_params=pltpu.CompilerParams(vmem_limit_bytes=63 * 2**20),
        cost_estimate=pl.CostEstimate(
            flops=25 * 10**9, bytes_accessed=30 * 10**6, transcendentals=2 * 10**6
        ),
        name="ffn",
    )(where, pack_f, x_t, o_t, cot_t, gain)


def attn_bwd_kernel(
    handed, cos_ref, sin_ref, q_t_ref, k_t_ref, v_t_ref, p_ref, o_t_ref, do_t_ref, *rest
):
    dqkv_ref = rest[handed]
    dq_ref, v_ref = rest[-2:]
    for group in range(KV_HEADS):
        v_ref[group] = v_t_ref[0, group * HEAD : (group + 1) * HEAD, :].astype(F32).T.astype(BF16)

    def group_step(group, carry):
        kv_rows = pl.ds(pl.multiple_of(group * HEAD, HEAD), HEAD)
        dk = [jnp.zeros((HEAD, HALF), F32) for _ in range(2)]
        dv = [jnp.zeros((HEAD, HALF), F32) for _ in range(2)]
        for member in range(HEADS // KV_HEADS):
            head = group * (HEADS // KV_HEADS) + member
            rows = pl.ds(pl.multiple_of(head * HEAD, HEAD), HEAD)
            for block in range(2):
                cols = slice(block * HALF, (block + 1) * HALF)
                keys = slice(0, (block + 1) * HALF)
                do_t = do_t_ref[0, rows, cols]
                q_t = q_t_ref[0, rows, cols]
                p_t = p_ref[0, head, keys, cols]
                row_sum = jnp.sum(
                    do_t.astype(F32) * o_t_ref[0, rows, cols].astype(F32), axis=0, keepdims=True
                )
                dp_t = mm(v_ref[group, keys, :], do_t)
                ds_t = (p_t.astype(F32) * (dp_t - row_sum)).astype(BF16)
                dq_ref[rows, cols] = mm(k_t_ref[0, kv_rows, keys], ds_t) * 0.125
                dk_new = mm(q_t, ds_t, NT)
                dv_new = mm(do_t, p_t, NT)
                for part in range(block + 1):
                    at = slice(part * HALF, (part + 1) * HALF)
                    dk[part] += dk_new[:, at]
                    dv[part] += dv_new[:, at]
        dq_ref[pl.ds(pl.multiple_of(D + group * HEAD, HEAD), HEAD), :] = jnp.concatenate(dk, axis=1)
        dqkv_ref[pl.ds(pl.multiple_of(D + KVW + group * HEAD, HEAD), HEAD), :] = jnp.concatenate(
            dv, axis=1
        ).astype(BF16)
        return carry

    lax.fori_loop(0, KV_HEADS, group_step, 0)
    dqkv_ref[: D + KVW] = rope_rows(
        dq_ref[...], cos_ref[0], sin_ref[0], HEADS + KV_HEADS, -1
    ).astype(BF16)


def attn_bwd(seq, args, handed):
    handed = list(handed)
    count = len(handed)
    hbm = pl.BlockSpec(memory_space=pl.ANY)
    return pl.pallas_call(
        functools.partial(attn_bwd_kernel, count),
        grid=(1,),
        in_specs=[
            seq_spec((32, SEQ), seq),
            seq_spec((32, SEQ), seq),
            seq_spec((D, SEQ), seq),
            seq_spec((KVW, SEQ), seq),
            seq_spec((KVW, SEQ), seq),
            seq_spec((HEADS, SEQ, SEQ), seq),
            seq_spec((D, SEQ), seq),
            seq_spec((D, SEQ), seq),
        ]
        + [hbm] * count,
        out_specs=[whole_spec((QKV, SEQ))] + [hbm] * count,
        out_shape=[jax.ShapeDtypeStruct((QKV, SEQ), BF16)]
        + [jax.ShapeDtypeStruct(v.shape, v.dtype) for v in handed],
        input_output_aliases={len(args) + k: 1 + k for k in range(count)},
        scratch_shapes=[
            pltpu.VMEM((D + KVW, SEQ), F32),
            pltpu.VMEM((KV_HEADS, SEQ, HEAD), BF16),
        ],
        compiler_params=pltpu.CompilerParams(vmem_limit_bytes=63 * 2**20),
        cost_estimate=pl.CostEstimate(flops=8 * 10**9, bytes_accessed=8 * 10**6, transcendentals=0),
        name="attn_bwd",
    )(*args, *handed)


def qkv_bwd_kernel(
    handed, where_ref, w_ref, gain_ref, dgain_two_ref, x_ref, h_t_ref, dx1_ref, dqkv0_ref, dqkv1_ref, *rest
):
    gx_ref, send_ref, keep_ref = rest[handed : handed + 3]
    dw_ref, dgain_ref, qs_ref, ks_ref, vs_ref, gs_ref, stage_ref = rest[-7:]
    dw = jnp.zeros((D, QKV), F32)
    dgain = jnp.zeros((D, 1), F32)
    for seq, dqkv_ref in enumerate((dqkv0_ref, dqkv1_ref)):
        dqkv = dqkv_ref[...]
        dh = mm(w_ref[...], dqkv)
        dw += mm(h_t_ref[seq], dqkv, NT)
        x = x_ref[seq].astype(F32)
        inv = lax.rsqrt(jnp.mean(x * x, axis=0, keepdims=True) + EPSILON)
        normed = x * inv
        dn = dh * gain_ref[:D]
        gx_ref[seq] = dx1_ref[seq] + inv * (
            dn - normed * jnp.mean(dn * normed, axis=0, keepdims=True)
        )
        dgain += jnp.sum(dh * normed, axis=1, keepdims=True)
    dw_ref[...] = dw
    dgain_ref[:D] = dgain
    dgain_ref[D:] = dgain_two_ref[...]
    join_square(qs_ref, dw_ref)
    for half in range(2):
        at = D + 96 * half
        ks_ref[pl.ds(half, D, stride=2), :96] = dw_ref[:, at : at + 96]
        vs_ref[pl.ds(half, D, stride=2), :96] = dw_ref[:, at + KVW : at + KVW + 96]
    for lane in range(9):
        gs_ref[:, lane : lane + 1] = dgain_ref[pl.ds(lane, 2 * CHIPS, stride=9), :]
    core = where_ref[0]
    stage_ref[...] = jnp.zeros_like(stage_ref)

    def spread(slot, carry):
        chip = chip_of(slot, where_ref, False)
        for keep_it in range(2):
            dev = chip * 2 + (core if keep_it else 1 - core)
            stage_ref[Q_QUERY : Q_QUERY + R_OUT, :] = get_rows(qs_ref, dev, R_OUT)
            stage_ref[Q_KEY : Q_KEY + R_KEY, :] = get_rows(ks_ref, dev, R_KEY)
            stage_ref[Q_VALUE : Q_VALUE + R_KEY, :] = get_rows(vs_ref, dev, R_KEY)
            stage_ref[Q_GAIN : Q_GAIN + 1, :] = get_rows(gs_ref, dev, 1)
            (keep_ref if keep_it else send_ref)[slot] = stage_ref[...].astype(BF16)
        return carry

    lax.fori_loop(0, CHIPS, spread, 0)


def qkv_bwd(args, handed):
    handed = list(handed)
    count = len(handed)
    hbm = pl.BlockSpec(memory_space=pl.ANY)
    seqs = args[4].shape[0]
    vmem = pl.BlockSpec(memory_space=pltpu.VMEM)
    return pl.pallas_call(
        functools.partial(qkv_bwd_kernel, count),
        in_specs=[pl.BlockSpec(memory_space=pltpu.SMEM)]
        + [vmem] * (len(args) - 1)
        + [hbm] * count,
        out_specs=[vmem] * 3 + [hbm] * count,
        out_shape=[
            jax.ShapeDtypeStruct((seqs, D, SEQ), F32),
            jax.ShapeDtypeStruct((CHIPS, ROWS_Q, 128), BF16),
            jax.ShapeDtypeStruct((CHIPS, ROWS_Q, 128), BF16),
        ]
        + [jax.ShapeDtypeStruct(v.shape, v.dtype) for v in handed],
        input_output_aliases={len(args) + k: 3 + k for k in range(count)},
        scratch_shapes=[
            pltpu.VMEM((D, QKV), F32),
            pltpu.VMEM((2 * D, 1), F32),
            pltpu.VMEM((2 * CHIPS * R_OUT, 128), F32),
            pltpu.VMEM((2 * CHIPS * R_KEY, 128), F32),
            pltpu.VMEM((2 * CHIPS * R_KEY, 128), F32),
            pltpu.VMEM((2 * CHIPS, 128), F32),
            pltpu.VMEM((ROWS_Q, 128), F32),
        ],
        compiler_params=pltpu.CompilerParams(vmem_limit_bytes=63 * 2**20),
        cost_estimate=pl.CostEstimate(flops=8 * 10**9, bytes_accessed=12 * 10**6, transcendentals=0),
        name="qkv_bwd",
    )(*args, *handed)


def pairs(axis, step):
    out = []
    for x in range(4):
        for y in range(4):
            for z in range(4):
                for core in range(2):
                    to = {"x": x, "y": y, "z": z, "c": core}
                    to[axis] = (to[axis] + step) % (2 if axis == "c" else 4)
                    me = ((x * 4 + y) * 4 + z) * 2 + core
                    out.append((me, ((to["x"] * 4 + to["y"]) * 4 + to["z"]) * 2 + to["c"]))
    return out


def hop(v, axis, step):
    return lax.ppermute(v, "dp", pairs(axis, step))


def sum_near(v, axis):
    low = v[1:].astype(BF16)
    got = [hop(low[k - 1], axis, k) for k in (2, 1, 3)]
    total = v[0].astype(F32)
    for piece in got:
        total = total + piece.astype(F32)
    return total


def ring_far(far, axis):
    cut = far.shape[0] // 2
    return hop(far[:cut], axis, 1).astype(F32), hop(far[cut:], axis, 3).astype(F32)


def ring_near(near, got, axis):
    cut = near.shape[1] // 2
    ahead = jnp.concatenate([near[0][:cut] + got[0], near[0][cut:]]).astype(BF16)
    behind = jnp.concatenate([near[1][:cut], near[1][cut:] + got[1]]).astype(BF16)
    return hop(ahead, axis, 1).astype(F32) + hop(behind, axis, 3).astype(F32)


def on_device(
    tokens, positions, norm_gains, w_query, w_key, w_value, w_out, w_gate, w_up, w_down, cotangent
):
    me = lax.axis_index("dp").astype(jnp.int32)
    where = jnp.stack([me % 2, me // 32, (me // 8) % 4, (me // 2) % 4])
    seqs = tokens.shape[0]
    x_t = jnp.swapaxes(tokens, 1, 2)
    cot_t = jnp.swapaxes(cotangent, 1, 2)

    pack_f, pack_q = pack(
        [
            lane_rows(jnp.concatenate([w_query, w_out]), 18, 288),
            jnp.concatenate([w_key, w_value]).reshape(18, 96),
            norm_gains.reshape(1, 9),
            lane_rows(w_down, 12, D),
            jnp.concatenate([w_gate, w_up]).reshape(2 * R_GATE, 128),
        ]
    )
    all_f = lax.all_gather(pack_f, "dp", axis=0, tiled=False)
    all_q = lax.all_to_all(
        jnp.broadcast_to(pack_q[None], (2 * CHIPS, ROWS_Q, 128)), "dp", split_axis=0, concat_axis=0
    )

    freqs = 100000.0 ** (-(jnp.arange(HEAD // 2, dtype=F32) * 2.0 / HEAD))
    angles = positions.astype(F32)[:, None, :] * freqs[None, :, None]
    cos_t = jnp.cos(angles)
    sin_t = jnp.sin(angles)
    fresh = (positions[:, 1:] != positions[:, :-1] + 1).astype(jnp.int32)
    docs = jnp.cumsum(jnp.pad(fresh, ((0, 0), (1, 0))), axis=1)

    wqkv, gain, h_t, q_t, k_t, v_t, p, o_t = attn_fwd(
        all_q, x_t, cos_t, sin_t, docs[:, None, :], docs[:, :, None]
    )
    y_t, dx1, do_t, dgain_two, send_g, keep_g, send_b, keep_b = ffn(
        where, all_f, x_t, o_t, cot_t, gain
    )
    got_g = hop(send_g, "c", 1)
    got_b = hop(send_b, "c", 1)
    args = [cos_t, sin_t, q_t, k_t, v_t, p, o_t, do_t]
    dqkv0, keep_g, keep_b = attn_bwd(0, args, [keep_g, keep_b])

    def halves(keep, got, rows):
        v = (keep.astype(F32) + got.astype(F32)).reshape(4, 4, 4, rows, 128)
        return v[2].astype(BF16), jnp.stack([v[1], v[3]]), v[0]

    far_g, near_g, own_g = halves(keep_g, got_g, ROWS_G)
    far_b, near_b, own_b = halves(keep_b, got_b, ROWS_B)
    got_g = ring_far(far_g, "z")
    got_b = ring_far(far_b, "y")
    dqkv1, near_g, near_b = attn_bwd(1, args, [near_g, near_b])
    sum_g = ring_near(near_g, got_g, "z")
    sum_b = ring_near(near_b, got_b, "y")
    gx_t, send_q, keep_q, own_g, own_b = qkv_bwd(
        [where, wqkv, gain, dgain_two, x_t, h_t, dx1, dqkv0, dqkv1], [own_g, own_b]
    )
    got_q = hop(send_q, "c", 1)
    sum_g = sum_g + own_g
    sum_b = sum_b + own_b
    sum_q = (keep_q.astype(F32) + got_q.astype(F32)).reshape(4, 4, 4, ROWS_Q, 128)
    sum_q = sum_near(sum_q, "z")
    sum_b = sum_near(sum_b, "z")
    sum_a = sum_near(jnp.concatenate([sum_g, sum_q], axis=2), "y")
    final = sum_near(jnp.concatenate([sum_a, sum_b], axis=1), "x")
    fg = final[:ROWS_G]
    fq = final[ROWS_G : ROWS_G + ROWS_Q]
    fb = final[ROWS_G + ROWS_Q :]
    return (
        jnp.swapaxes(y_t, 1, 2),
        jnp.swapaxes(gx_t, 1, 2),
        take_lanes(fq[Q_GAIN : Q_GAIN + 1], 1, 9),
        take_lanes(fq[Q_QUERY : Q_QUERY + R_OUT], 9, 288),
        take_lanes(fq[Q_KEY : Q_KEY + R_KEY], 9, 96),
        take_lanes(fq[Q_VALUE : Q_VALUE + R_KEY], 9, 96),
        take_lanes(fg[G_OUT : G_OUT + R_OUT], 9, 288),
        fb[B_GATE : B_GATE + R_GATE].reshape(-1),
        fb[B_UP : B_UP + R_GATE].reshape(-1),
        take_lanes(fg[G_DOWN : G_DOWN + R_DOWN], 12, D),
    )


def solution(mesh):
    flat = P("dp")
    cube = P("dp", None, None)
    return jax.shard_map(
        on_device,
        mesh=mesh,
        in_specs=(cube, P("dp", None)) + (flat,) * 8 + (cube,),
        out_specs=(cube, cube) + (flat,) * 8,
        check_vma=False,
    )
```

profile of v0, /device:TPU:0, one launch (start us, length us, event | category | flops | bytes accessed | tf_op | source)
XLA Modules:
  0.0 263.3 jit_solution(5723870482884747850)
XLA Ops:
  11.0 0.8 reshape.177
  13.0 1.3 pad_maximum_fusion.8.wgu
  14.4 1.4 pack.1
  15.8 2.1 broadcast_in_dim.2
  17.9 11.6 %all-to-all-start = ((bf16[128,48,128]{2,1,0:T(8,128)(2,1)}), bf16[128,48,128]{2,1,0:T(8,128)(2,1)}, u32[]{:S(2)}, u32[]{:S(2)}) async-start(bf16[128,48,128]{2,1,0:T(8,128)(2,1)} %broadcast_in_dim.2), calls=%async_computation | async-start | bytes 3145728 | tf_op jit(solution)/shard_map/all_to_all | solution.py:626
  30.8 1.2 reduce_window_sum.34.docc_ref
  32.6 1.2 multiply_sine_fusion
  33.8 20.8 %all-to-all-done.pack_ref = bf16[128,48,128]{2,1,0:T(8,128)(2,1)} async-done(((bf16[128,48,128]{2,1,0:T(8,128)(2,1)}), bf16[128,48,128]{2,1,0:T(8,128)(2,1)}, u32[]{:S(2)}, u32[]{:S(2)}) %all-to-all-start) | async-done | bytes 1572896 | tf_op jit(solution)/shard_map/all_to_all | solution.py:626
  54.6 22.8 %attn_fwd.1 = (bf16[576,960]{1,0:T(8,128)(2,1)}, f32[1152,1]{1,0:T(8,128)}, bf16[2,576,512]{2,1,0:T(8,128)(2,1)}, bf16[2,576,512]{2,1,0:T(8,128)(2,1)}, bf16[2,1...) custom-call(bf16[128,48,128]{2,1,0:T(8,128)(2,1)} %all-to-all-done.p, ...), custom_call_target="tpu_custom_call" | custom-call | flops 8000000000 | bytes 20000000 | tf_op jit(solution)/shard_map/attn_fwd/pallas_call | solution.py:223
  77.4 21.5 %all-gather.3.cloned.1.call-done = bf16[26624,128]{1,0:T(8,128)(2,1)} async-done(((bf16[208,128]{1,0:T(8,128)(2,1)}), bf16[26624,128]{1,0:T(8,128)(2,1)}) %all-gather.3.cloned.1.call-update) | async-done | bytes 6815760 | tf_op jit(solution)/shard_map/all_gather | solution.py:625
  98.9 41.1 %ffn.1 = (bf16[2,576,512]{2,1,0:T(8,128)(2,1)}, f32[2,576,512]{2,1,0:T(8,128)}, bf16[2,576,512]{2,1,0:T(8,128)(2,1)}, f32[576,1]{1,0:T(8,128)}, bf16[64,96,128]{...) custom-call(s32[4]{0:T(128)} %pad_add_fusion.where_ref, ...), custom_call_target="tpu_custom_call" | custom-call | flops 24999999488 | bytes 30000000 | tf_op jit(solution)/shard_map/ffn/pallas_call | solution.py:374
  140.6 9.9 %attn_bwd.2 = (bf16[960,512]{1,0:T(8,128)(2,1)}, bf16[64,96,128]{2,1,0:T(8,128)(2,1)}, bf16[64,112,128]{2,1,0:T(8,128)(2,1)}) custom-call(f32[2,32,512]{2,1,0:T(8,128)} %get-tuple-element.113.cos_ref, f32[2,32,512]{2,1,0:T(8,128)} %get-tuple-element.112.sin_ref, ...), custom_call_target="tpu_custom_call", output_to_operand_aliasing={{1}: (8, {}), {2}: (9, {})} | custom-call | flops 8000000000 | bytes 8000000 | tf_op jit(solution)/shard_map/attn_bwd/pallas_call | solution.py:461
  150.4 2.5 fusion.23
  154.4 1.3 collective-permute-start.2
  155.7 1.0 fusion.27
  156.8 1.4 pad_maximum_fusion.1.rest_0_
  158.8 2.0 fusion.24
  160.8 0.8 fusion.28
  161.6 1.4 collective-permute-start.15
  163.6 1.2 fusion.26
  164.8 1.4 pad_maximum_fusion.rest_1_
  166.2 9.9 %attn_bwd.3 = (bf16[960,512]{1,0:T(8,128)(2,1)}, f32[2,4,4,96,128]{4,3,2,1,0:T(8,128)}, f32[2,4,4,112,128]{4,3,2,1,0:T(8,128)}) custom-call(f32[2,32,512]{2,1,0:T(8,128)} %get-tuple-element.113.cos_ref, f32[2,32,512]{2,1,0:T(8,128)} %get-tuple-element.112.sin_ref, ...), custom_call_target="tpu_custom_call", output_to_operand_aliasing={{1}: (8, {}), {2}: (9, {})} | custom-call | flops 8000000000 | bytes 8000000 | tf_op jit(solution)/shard_map/attn_bwd/pallas_call | solution.py:461
  176.1 1.6 convert.54
  178.2 1.2 copy-done.1
  179.5 1.1 fusion.5
  181.4 2.6 %collective-permute-start.5 = (bf16[4,4,96,128]{3,2,1,0:T(8,128)(2,1)}, bf16[4,4,96,128]{3,2,1,0:T(8,128)(2,1)}, u32[]{:S(2)}, u32[]{:S(2)}) collective-permute-start(bf16[4,4,96,128]{3,2,1,0:T(8,128)(2,1)} %pad_maximum_fusion.7), channel_id=1, source_target_pairs={{0,6},{1,7},{2,0},{3,1},{4,2},{5,3},{6,4},{7,5},{8,14},{9,15},{10,... | collective-permute-start | bytes 1179656 | tf_op jit(solution)/shard_map/ppermute | solution.py:583
  184.0 0.8 pad_maximum_fusion.6
  184.8 12.1 %qkv_bwd.1 = (f32[2,576,512]{2,1,0:T(8,128)}, bf16[64,48,128]{2,1,0:T(8,128)(2,1)}, bf16[64,48,128]{2,1,0:T(8,128)(2,1)}, f32[4,4,96,128]{3,2,1,0:T(8,128)}, f32[4,4,112,128]{3,2,1,0:T(8,128)}) custom-call(s32[4]{0:T(128)} %pad_add_fusion.where_ref, bf16[576,960]{1,0:T(8,128)(2,1)} %get-tuple-element.44.w_ref, ...), custom_call_target="tpu_custom_call", output_to_operand_aliasing={{3}: (9, {}), {4}: (10, {})} | custom-call | flops 8000000000 | bytes 12000000 | tf_op jit(solution)/shard_map/qkv_bwd/pallas_call | solution.py:541
  197.0 1.5 fusion.3
  198.5 3.3 %collective-permute-start.16 = (bf16[4,4,112,128]{3,2,1,0:T(8,128)(2,1)S(1)}, bf16[4,4,112,128]{3,2,1,0:T(8,128)(2,1)S(1)}, u32[]{:S(2)}, u32[]{:S(2)}) collective-permute-start(bf16[4,4,112,128]{3,2,1,0:T(8,128)(2,1)S(1)} %pad_maximum_fusion.5), channel_id=1, source_target_pairs={{0,24},{1,25},{2,26},{3,27},{4,28},{5,29},{6,30},{7,31},{8,0},{9,1... | collective-permute-start | bytes 1376264 | tf_op jit(solution)/shard_map/ppermute | solution.py:583
  202.0 1.3 add_add_fusion.1
  203.3 8.9 %collective-permute-done.16 = bf16[4,4,112,128]{3,2,1,0:T(8,128)(2,1)S(1)} collective-permute-done((bf16[4,4,112,128]{3,2,1,0:T(8,128)(2,1)S(1)}, bf16[4,4,112,128]{3,2,1,0:T(8,128)(2,1)S(1)}, u32[]{:S(2)}, u32[]{:S(2)}) %collective-permute-start.16) | collective-permute-done | bytes 458784 | tf_op jit(solution)/shard_map/ppermute | solution.py:583
  212.3 3.5 %collective-permute-done.14 = bf16[4,4,112,128]{3,2,1,0:T(8,128)(2,1)S(1)} collective-permute-done((bf16[4,4,112,128]{3,2,1,0:T(8,128)(2,1)S(1)}, bf16[4,4,112,128]{3,2,1,0:T(8,128)(2,1)S(1)}, u32[]{:S(2)}, u32[]{:S(2)}) %collective-permute-start.14) | collective-permute-done | bytes 458784 | tf_op jit(solution)/shard_map/ppermute | solution.py:583
  216.0 1.0 copy-done.5
  217.2 3.3 %collective-permute-start.9 = (bf16[4,4,48,128]{3,2,1,0:T(8,128)(2,1)S(1)}, bf16[4,4,48,128]{3,2,1,0:T(8,128)(2,1)S(1)}, u32[]{:S(2)}, u32[]{:S(2)}) collective-permute-start(bf16[4,4,48,128]{3,2,1,0:T(8,128)(2,1)S(1)} %bitcast.112), channel_id=1, source_target_pairs={{0,6},{1,7},{2,0},{3,1},{4,2},{5,3},{6,4},{7,5},{8,14},{9,15},{10,... | collective-permute-start | bytes 589832 | tf_op jit(solution)/shard_map/ppermute | solution.py:583
  220.5 0.9 collective-permute-start.8
  221.4 2.7 %collective-permute-start.17 = (bf16[4,112,128]{2,1,0:T(8,128)(2,1)S(1)}, bf16[4,112,128]{2,1,0:T(8,128)(2,1)S(1)}, u32[]{:S(2)}, u32[]{:S(2)}) collective-permute-start(bf16[4,112,128]{2,1,0:T(8,128)(2,1)S(1)} %get-tuple-element.100), channel_id=1, source_target_pairs={{0,4},{1,5},{2,6},{3,7},{4,0},{5,1},{6,2},{7,3},{8,12},{9,13},{10,... | collective-permute-start | bytes 344072 | tf_op jit(solution)/shard_map/ppermute | solution.py:583
  224.1 2.6 collective-permute-start.19
  226.8 5.4 %collective-permute-done.9 = bf16[4,4,48,128]{3,2,1,0:T(8,128)(2,1)S(1)} collective-permute-done((bf16[4,4,48,128]{3,2,1,0:T(8,128)(2,1)S(1)}, bf16[4,4,48,128]{3,2,1,0:T(8,128)(2,1)S(1)}, u32[]{:S(2)}, u32[]{:S(2)}) %collective-permute-start.9) | collective-permute-done | bytes 196640 | tf_op jit(solution)/shard_map/ppermute | solution.py:583
  232.1 0.9 collective-permute-done.8
  233.4 2.0 collective-permute-start.12
  235.5 3.1 %collective-permute-done.18 = bf16[4,112,128]{2,1,0:T(8,128)(2,1)S(1)} collective-permute-done((bf16[4,112,128]{2,1,0:T(8,128)(2,1)S(1)}, bf16[4,112,128]{2,1,0:T(8,128)(2,1)S(1)}, u32[]{:S(2)}, u32[]{:S(2)}) %collective-permute-start.18) | collective-permute-done | bytes 114720 | tf_op jit(solution)/shard_map/ppermute | solution.py:583
  238.6 3.0 %collective-permute-done.10 = bf16[4,144,128]{2,1,0:T(8,128)(2,1)S(1)} collective-permute-done((bf16[4,144,128]{2,1,0:T(8,128)(2,1)S(1)}, bf16[4,144,128]{2,1,0:T(8,128)(2,1)S(1)}, u32[]{:S(2)}, u32[]{:S(2)}) %collective-permute-start.10) | collective-permute-done | bytes 147488 | tf_op jit(solution)/shard_map/ppermute | solution.py:583
  241.7 1.6 collective-permute-done.11
  243.4 1.5 collective-permute-start.20
  245.0 1.5 collective-permute-start.22
  247.0 2.8 %collective-permute-done.20 = bf16[256,128]{1,0:T(8,128)(2,1)S(1)} collective-permute-done((bf16[256,128]{1,0:T(8,128)(2,1)S(1)}, bf16[256,128]{1,0:T(8,128)(2,1)S(1)}, u32[]{:S(2)}, u32[]{:S(2)}) %collective-permute-start.20) | collective-permute-done | bytes 65568 | tf_op jit(solution)/shard_map/ppermute | solution.py:583
  249.8 2.1 collective-permute-done.21
  (94 shorter events, 17.8 us)
Async XLA Ops:
  7.2 91.8 %all-gather.3.cloned.1.call-start = ((), (), s32[]{:S(2)}) async-start(), calls=%async_computation.1 | async-start | bytes 6868992 | tf_op jit(solution)/shard_map/all_gather | solution.py:625
  17.9 11.7 %copy-start.6 = (s32[2,512]{1,0:T(2,128)S(1)}, s32[2,512]{1,0:T(2,128)}, u32[]{:S(2)}) copy-start(s32[2,512]{1,0:T(2,128)} %param.12) | copy-start | bytes 12292
  17.9 36.7 %all-to-all-start = ((bf16[128,48,128]{2,1,0:T(8,128)(2,1)}), bf16[128,48,128]{2,1,0:T(8,128)(2,1)}, u32[]{:S(2)}, u32[]{:S(2)}) async-start(bf16[128,48,128]{2,1,0:T(8,128)(2,1)} %broadcast_in_dim.2), calls=%async_computation | async-start | bytes 3145728 | tf_op jit(solution)/shard_map/all_to_all | solution.py:626
  30.8 23.8 %copy-start.7 = (s32[2,4,128]{2,1,0:T(4,128)}, s32[2,4,128]{2,1,0:T(4,128)S(1)}, u32[]{:S(2)}) copy-start(s32[2,4,128]{2,1,0:T(4,128)S(1)} %broadcast_add_fusion) | copy-start | bytes 12292
  140.1 10.4 %collective-permute-start = (bf16[64,96,128]{2,1,0:T(8,128)(2,1)}, bf16[64,96,128]{2,1,0:T(8,128)(2,1)}, u32[]{:S(2)}, u32[]{:S(2)}) collective-permute-start(bf16[64,96,128]{2,1,0:T(8,128)(2,1)} %get-tuple-element.57), channel_id=1, source_target_pairs={{0,1},{1,0},{2,3},{3,2},{4,5},{5,4},{6,7},{7,6},{8,9},{9,8},{10,11... | collective-permute-start | bytes 4718600 | tf_op jit(solution)/shard_map/ppermute | solution.py:583
  140.3 17.8 %collective-permute-start.1 = (bf16[64,112,128]{2,1,0:T(8,128)(2,1)}, bf16[64,112,128]{2,1,0:T(8,128)(2,1)}, u32[]{:S(2)}, u32[]{:S(2)}) collective-permute-start(bf16[64,112,128]{2,1,0:T(8,128)(2,1)} %get-tuple-element.59), channel_id=1, source_target_pairs={{0,1},{1,0},{2,3},{3,2},{4,5},{5,4},{6,7},{7,6},{8,9},{9,8},{10,11... | collective-permute-start | bytes 5505032 | tf_op jit(solution)/shard_map/ppermute | solution.py:583
  153.7 24.5 %collective-permute-start.4 = (bf16[2,4,96,128]{3,2,1,0:T(8,128)(2,1)}, bf16[2,4,96,128]{3,2,1,0:T(8,128)(2,1)}, u32[]{:S(2)}, u32[]{:S(2)}) collective-permute-start(bf16[2,4,96,128]{3,2,1,0:T(8,128)(2,1)} %bitcast.24), channel_id=1, source_target_pairs={{0,6},{1,7},{2,0},{3,1},{4,2},{5,3},{6,4},{7,5},{8,14},{9,15},{10,... | collective-permute-start | bytes 589832 | tf_op jit(solution)/shard_map/ppermute | solution.py:583
  154.4 23.8 %collective-permute-start.2 = (bf16[2,4,96,128]{3,2,1,0:T(8,128)(2,1)}, bf16[2,4,96,128]{3,2,1,0:T(8,128)(2,1)}, u32[]{:S(2)}, u32[]{:S(2)}) collective-permute-start(bf16[2,4,96,128]{3,2,1,0:T(8,128)(2,1)} %bitcast.20), channel_id=1, source_target_pairs={{0,2},{1,3},{2,4},{3,5},{4,6},{5,7},{6,0},{7,1},{8,10},{9,11},{10,... | collective-permute-start | bytes 589832 | tf_op jit(solution)/shard_map/ppermute | solution.py:583
  156.8 2.1 copy-start.4
  161.6 35.3 %collective-permute-start.15 = (bf16[2,4,112,128]{3,2,1,0:T(8,128)(2,1)}, bf16[2,4,112,128]{3,2,1,0:T(8,128)(2,1)}, u32[]{:S(2)}, u32[]{:S(2)}) collective-permute-start(bf16[2,4,112,128]{3,2,1,0:T(8,128)(2,1)} %bitcast.38), channel_id=1, source_target_pairs={{0,24},{1,25},{2,26},{3,27},{4,28},{5,29},{6,30},{7,31},{8,0},{9,1... | collective-permute-start | bytes 688136 | tf_op jit(solution)/shard_map/ppermute | solution.py:583
  163.0 33.9 %collective-permute-start.13 = (bf16[2,4,112,128]{3,2,1,0:T(8,128)(2,1)}, bf16[2,4,112,128]{3,2,1,0:T(8,128)(2,1)}, u32[]{:S(2)}, u32[]{:S(2)}) collective-permute-start(bf16[2,4,112,128]{3,2,1,0:T(8,128)(2,1)} %bitcast.34), channel_id=1, source_target_pairs={{0,8},{1,9},{2,10},{3,11},{4,12},{5,13},{6,14},{7,15},{8,16},{9,17... | collective-permute-start | bytes 688136 | tf_op jit(solution)/shard_map/ppermute | solution.py:583
  176.1 2.0 copy-start
  178.1 1.4 copy-start.1
  181.4 20.6 %collective-permute-start.5 = (bf16[4,4,96,128]{3,2,1,0:T(8,128)(2,1)}, bf16[4,4,96,128]{3,2,1,0:T(8,128)(2,1)}, u32[]{:S(2)}, u32[]{:S(2)}) collective-permute-start(bf16[4,4,96,128]{3,2,1,0:T(8,128)(2,1)} %pad_maximum_fusion.7), channel_id=1, source_target_pairs={{0,6},{1,7},{2,0},{3,1},{4,2},{5,3},{6,4},{7,5},{8,14},{9,15},{10,... | collective-permute-start | bytes 1179656 | tf_op jit(solution)/shard_map/ppermute | solution.py:583
  184.8 17.1 %collective-permute-start.3 = (bf16[4,4,96,128]{3,2,1,0:T(8,128)(2,1)}, bf16[4,4,96,128]{3,2,1,0:T(8,128)(2,1)}, u32[]{:S(2)}, u32[]{:S(2)}) collective-permute-start(bf16[4,4,96,128]{3,2,1,0:T(8,128)(2,1)} %pad_maximum_fusion.6), channel_id=1, source_target_pairs={{0,2},{1,3},{2,4},{3,5},{4,6},{5,7},{6,0},{7,1},{8,10},{9,11},{10,... | collective-permute-start | bytes 1179656 | tf_op jit(solution)/shard_map/ppermute | solution.py:583
  196.9 19.1 %collective-permute-start.6 = (bf16[64,48,128]{2,1,0:T(8,128)(2,1)}, bf16[64,48,128]{2,1,0:T(8,128)(2,1)S(1)}, u32[]{:S(2)}, u32[]{:S(2)}) collective-permute-start(bf16[64,48,128]{2,1,0:T(8,128)(2,1)} %get-tuple-element.65), channel_id=1, source_target_pairs={{0,1},{1,0},{2,3},{3,2},{4,5},{5,4},{6,7},{7,6},{8,9},{9,8},{10,11... | collective-permute-start | bytes 2359304 | tf_op jit(solution)/shard_map/ppermute | solution.py:583
  196.9 5.0 %copy-start.3 = (f32[4,4,96,128]{3,2,1,0:T(8,128)S(1)}, f32[4,4,96,128]{3,2,1,0:T(8,128)}, u32[]{:S(2)}) copy-start(f32[4,4,96,128]{3,2,1,0:T(8,128)} %get-tuple-element.63) | copy-start | bytes 2359300
  198.5 13.8 %collective-permute-start.16 = (bf16[4,4,112,128]{3,2,1,0:T(8,128)(2,1)S(1)}, bf16[4,4,112,128]{3,2,1,0:T(8,128)(2,1)S(1)}, u32[]{:S(2)}, u32[]{:S(2)}) collective-permute-start(bf16[4,4,112,128]{3,2,1,0:T(8,128)(2,1)S(1)} %pad_maximum_fusion.5), channel_id=1, source_target_pairs={{0,24},{1,25},{2,26},{3,27},{4,28},{5,29},{6,30},{7,31},{8,0},{9,1... | collective-permute-start | bytes 1376264 | tf_op jit(solution)/shard_map/ppermute | solution.py:583
  201.8 14.0 %copy-start.2 = (f32[4,4,112,128]{3,2,1,0:T(8,128)S(1)}, f32[4,4,112,128]{3,2,1,0:T(8,128)}, u32[]{:S(2)}) copy-start(f32[4,4,112,128]{3,2,1,0:T(8,128)} %get-tuple-element.67) | copy-start | bytes 2752516
  201.8 13.9 %collective-permute-start.14 = (bf16[4,4,112,128]{3,2,1,0:T(8,128)(2,1)S(1)}, bf16[4,4,112,128]{3,2,1,0:T(8,128)(2,1)S(1)}, u32[]{:S(2)}, u32[]{:S(2)}) collective-permute-start(bf16[4,4,112,128]{3,2,1,0:T(8,128)(2,1)S(1)} %pad_maximum_fusion.4), channel_id=1, source_target_pairs={{0,8},{1,9},{2,10},{3,11},{4,12},{5,13},{6,14},{7,15},{8,16},{9,17... | collective-permute-start | bytes 1376264 | tf_op jit(solution)/shard_map/ppermute | solution.py:583
  215.8 1.1 copy-start.5
  217.2 15.0 %collective-permute-start.9 = (bf16[4,4,48,128]{3,2,1,0:T(8,128)(2,1)S(1)}, bf16[4,4,48,128]{3,2,1,0:T(8,128)(2,1)S(1)}, u32[]{:S(2)}, u32[]{:S(2)}) collective-permute-start(bf16[4,4,48,128]{3,2,1,0:T(8,128)(2,1)S(1)} %bitcast.112), channel_id=1, source_target_pairs={{0,6},{1,7},{2,0},{3,1},{4,2},{5,3},{6,4},{7,5},{8,14},{9,15},{10,... | collective-permute-start | bytes 589832 | tf_op jit(solution)/shard_map/ppermute | solution.py:583
  220.5 11.7 %collective-permute-start.7 = (bf16[4,4,48,128]{3,2,1,0:T(8,128)(2,1)S(1)}, bf16[4,4,48,128]{3,2,1,0:T(8,128)(2,1)S(1)}, u32[]{:S(2)}, u32[]{:S(2)}) collective-permute-start(bf16[4,4,48,128]{3,2,1,0:T(8,128)(2,1)S(1)} %bitcast.111), channel_id=1, source_target_pairs={{0,4},{1,5},{2,6},{3,7},{4,0},{5,1},{6,2},{7,3},{8,12},{9,13},{10,... | collective-permute-start | bytes 589832 | tf_op jit(solution)/shard_map/ppermute | solution.py:583
  220.5 12.6 %collective-permute-start.8 = (bf16[4,4,48,128]{3,2,1,0:T(8,128)(2,1)S(1)}, bf16[4,4,48,128]{3,2,1,0:T(8,128)(2,1)S(1)}, u32[]{:S(2)}, u32[]{:S(2)}) collective-permute-start(bf16[4,4,48,128]{3,2,1,0:T(8,128)(2,1)S(1)} %bitcast.110), channel_id=1, source_target_pairs={{0,2},{1,3},{2,4},{3,5},{4,6},{5,7},{6,0},{7,1},{8,10},{9,11},{10,... | collective-permute-start | bytes 589832 | tf_op jit(solution)/shard_map/ppermute | solution.py:583
  221.4 14.0 %collective-permute-start.17 = (bf16[4,112,128]{2,1,0:T(8,128)(2,1)S(1)}, bf16[4,112,128]{2,1,0:T(8,128)(2,1)S(1)}, u32[]{:S(2)}, u32[]{:S(2)}) collective-permute-start(bf16[4,112,128]{2,1,0:T(8,128)(2,1)S(1)} %get-tuple-element.100), channel_id=1, source_target_pairs={{0,4},{1,5},{2,6},{3,7},{4,0},{5,1},{6,2},{7,3},{8,12},{9,13},{10,... | collective-permute-start | bytes 344072 | tf_op jit(solution)/shard_map/ppermute | solution.py:583
  224.1 11.4 %collective-permute-start.19 = (bf16[4,112,128]{2,1,0:T(8,128)(2,1)S(1)}, bf16[4,112,128]{2,1,0:T(8,128)(2,1)S(1)}, u32[]{:S(2)}, u32[]{:S(2)}) collective-permute-start(bf16[4,112,128]{2,1,0:T(8,128)(2,1)S(1)} %get-tuple-element.101), channel_id=1, source_target_pairs={{0,6},{1,7},{2,0},{3,1},{4,2},{5,3},{6,4},{7,5},{8,14},{9,15},{10,... | collective-permute-start | bytes 344072 | tf_op jit(solution)/shard_map/ppermute | solution.py:583
  232.1 6.4 %collective-permute-start.18 = (bf16[4,112,128]{2,1,0:T(8,128)(2,1)S(1)}, bf16[4,112,128]{2,1,0:T(8,128)(2,1)S(1)}, u32[]{:S(2)}, u32[]{:S(2)}) collective-permute-start(bf16[4,112,128]{2,1,0:T(8,128)(2,1)S(1)} %get-tuple-element.102), channel_id=1, source_target_pairs={{0,2},{1,3},{2,4},{3,5},{4,6},{5,7},{6,0},{7,1},{8,10},{9,11},{10,... | collective-permute-start | bytes 344072 | tf_op jit(solution)/shard_map/ppermute | solution.py:583
  233.3 8.4 %collective-permute-start.10 = (bf16[4,144,128]{2,1,0:T(8,128)(2,1)S(1)}, bf16[4,144,128]{2,1,0:T(8,128)(2,1)S(1)}, u32[]{:S(2)}, u32[]{:S(2)}) collective-permute-start(bf16[4,144,128]{2,1,0:T(8,128)(2,1)S(1)} %get-tuple-element.97), channel_id=1, source_target_pairs={{0,16},{1,17},{2,18},{3,19},{4,20},{5,21},{6,22},{7,23},{8,24},{9,... | collective-permute-start | bytes 442376 | tf_op jit(solution)/shard_map/ppermute | solution.py:583
  233.4 8.3 %collective-permute-start.12 = (bf16[4,144,128]{2,1,0:T(8,128)(2,1)S(1)}, bf16[4,144,128]{2,1,0:T(8,128)(2,1)S(1)}, u32[]{:S(2)}, u32[]{:S(2)}) collective-permute-start(bf16[4,144,128]{2,1,0:T(8,128)(2,1)S(1)} %get-tuple-element.98), channel_id=1, source_target_pairs={{0,24},{1,25},{2,26},{3,27},{4,28},{5,29},{6,30},{7,31},{8,0},{9,1... | collective-permute-start | bytes 442376 | tf_op jit(solution)/shard_map/ppermute | solution.py:583
  235.4 7.9 %collective-permute-start.11 = (bf16[4,144,128]{2,1,0:T(8,128)(2,1)S(1)}, bf16[4,144,128]{2,1,0:T(8,128)(2,1)S(1)}, u32[]{:S(2)}, u32[]{:S(2)}) collective-permute-start(bf16[4,144,128]{2,1,0:T(8,128)(2,1)S(1)} %get-tuple-element.99), channel_id=1, source_target_pairs={{0,8},{1,9},{2,10},{3,11},{4,12},{5,13},{6,14},{7,15},{8,16},{9,17... | collective-permute-start | bytes 442376 | tf_op jit(solution)/shard_map/ppermute | solution.py:583
  243.4 6.4 %collective-permute-start.20 = (bf16[256,128]{1,0:T(8,128)(2,1)S(1)}, bf16[256,128]{1,0:T(8,128)(2,1)S(1)}, u32[]{:S(2)}, u32[]{:S(2)}) collective-permute-start(bf16[256,128]{1,0:T(8,128)(2,1)S(1)} %get-tuple-element.103), channel_id=1, source_target_pairs={{0,64},{1,65},{2,66},{3,67},{4,68},{5,69},{6,70},{7,71},{8,72},{9,... | collective-permute-start | bytes 196616 | tf_op jit(solution)/shard_map/ppermute | solution.py:583
  245.0 4.9 %collective-permute-start.22 = (bf16[256,128]{1,0:T(8,128)(2,1)S(1)}, bf16[256,128]{1,0:T(8,128)(2,1)S(1)}, u32[]{:S(2)}, u32[]{:S(2)}) collective-permute-start(bf16[256,128]{1,0:T(8,128)(2,1)S(1)} %get-tuple-element.104), channel_id=1, source_target_pairs={{0,96},{1,97},{2,98},{3,99},{4,100},{5,101},{6,102},{7,103},{8,104... | collective-permute-start | bytes 196616 | tf_op jit(solution)/shard_map/ppermute | solution.py:583
  246.4 5.5 %collective-permute-start.21 = (bf16[256,128]{1,0:T(8,128)(2,1)S(1)}, bf16[256,128]{1,0:T(8,128)(2,1)S(1)}, u32[]{:S(2)}, u32[]{:S(2)}) collective-permute-start(bf16[256,128]{1,0:T(8,128)(2,1)S(1)} %get-tuple-element.105), channel_id=1, source_target_pairs={{0,32},{1,33},{2,34},{3,35},{4,36},{5,37},{6,38},{7,39},{8,40},{9,... | collective-permute-start | bytes 196616 | tf_op jit(solution)/shard_map/ppermute | solution.py:583
Sparse Core Ops, SparseCore 0:
  15.9 82.9 all-gather.2
where the time goes:
time: 264 us; the launch traced here: 263 us
  Pallas kernels  97.2 us (37%)
  waiting for transfers between devices  73.7 us (28%)
  starting transfers between devices  37.5 us (14%)
  local copies, waits for them, and re-layouts  20.4 us (8%)
  other arithmetic  20.1 us (8%)
  between operations  14.4 us (5%)
    pallas_call x1, Pallas kernels, ffn(): pl.pallas_call(ffn_kernel, in_specs=[pl.BlockSpec(memory_space=pltpu.SMEM...  41.1 us
    ppermute x23, waiting for transfers between devices, hop(): return lax.ppermute(v, 'dp', pairs(axis, step))  31.4 us
    ppermute x23, starting transfers between devices, hop(): return lax.ppermute(v, 'dp', pairs(axis, step))  25.9 us
    pallas_call x1, Pallas kernels, attn_fwd(): pl.pallas_call(attn_fwd_kernel, grid=(seqs,), in_specs=[whole_spec((2 * C...  22.8 us
    all_gather x1, waiting for transfers between devices, on_device(): all_f = lax.all_gather(pack_f, 'dp', axis=0, tiled=False)  21.5 us
    all_to_all x1, waiting for transfers between devices, on_device(): lax.all_to_all(jnp.broadcast_to(pack_q[None], (2 * CHIPS, ROWS_Q, 128)),...  20.8 us
    pallas_call x2, Pallas kernels, attn_bwd(): pl.pallas_call(functools.partial(attn_bwd_kernel, count), grid=(1,), in_s...  19.7 us
    pallas_call x1, Pallas kernels, qkv_bwd(): pl.pallas_call(functools.partial(qkv_bwd_kernel, count), in_specs=[pl.Blo...  12.1 us
  transfers between devices with their start and end apart: 25, of which 11 were waited for; matrix products, arithmetic and copies ran while one was open for 10% of the time, Pallas kernels for 21%

commit v1 on v0

--- a/solution.py
+++ b/solution.py
@@ -1,5 +1,3 @@
-import functools
-
 import jax
 import jax.numpy as jnp
 from jax import lax
@@ -410,10 +408,10 @@
 
 
 def attn_bwd_kernel(
-    handed, cos_ref, sin_ref, q_t_ref, k_t_ref, v_t_ref, p_ref, o_t_ref, do_t_ref, *rest
+    cos_ref, sin_ref, q_t_ref, k_t_ref, v_t_ref, p_ref, o_t_ref, do_t_ref, *rest
 ):
-    dqkv_ref = rest[handed]
-    dq_ref, v_ref = rest[-2:]
+    dqkv_ref, zero_ref, dq_ref, v_ref = rest[-4:]
+    zero_ref[...] = jnp.zeros_like(zero_ref)
     for group in range(KV_HEADS):
         v_ref[group] = v_t_ref[0, group * HEAD : (group + 1) * HEAD, :].astype(F32).T.astype(BF16)
 
@@ -454,12 +452,9 @@
     ).astype(BF16)
 
 
-def attn_bwd(seq, args, handed):
-    handed = list(handed)
-    count = len(handed)
-    hbm = pl.BlockSpec(memory_space=pl.ANY)
+def attn_bwd(seq, args, after):
     return pl.pallas_call(
-        functools.partial(attn_bwd_kernel, count),
+        attn_bwd_kernel,
         grid=(1,),
         in_specs=[
             seq_spec((32, SEQ), seq),
@@ -471,11 +466,12 @@
             seq_spec((D, SEQ), seq),
             seq_spec((D, SEQ), seq),
         ]
-        + [hbm] * count,
-        out_specs=[whole_spec((QKV, SEQ))] + [hbm] * count,
-        out_shape=[jax.ShapeDtypeStruct((QKV, SEQ), BF16)]
-        + [jax.ShapeDtypeStruct(v.shape, v.dtype) for v in handed],
-        input_output_aliases={len(args) + k: 1 + k for k in range(count)},
+        + [pl.BlockSpec(memory_space=pl.ANY)] * len(after),
+        out_specs=[whole_spec((QKV, SEQ)), whole_spec((8, 128))],
+        out_shape=[
+            jax.ShapeDtypeStruct((QKV, SEQ), BF16),
+            jax.ShapeDtypeStruct((8, 128), F32),
+        ],
         scratch_shapes=[
             pltpu.VMEM((D + KVW, SEQ), F32),
             pltpu.VMEM((KV_HEADS, SEQ, HEAD), BF16),
@@ -483,14 +479,15 @@
         compiler_params=pltpu.CompilerParams(vmem_limit_bytes=63 * 2**20),
         cost_estimate=pl.CostEstimate(flops=8 * 10**9, bytes_accessed=8 * 10**6, transcendentals=0),
         name="attn_bwd",
-    )(*args, *handed)
+    )(*args, *after)
 
 
 def qkv_bwd_kernel(
-    handed, where_ref, w_ref, gain_ref, dgain_two_ref, x_ref, h_t_ref, dx1_ref, dqkv0_ref, dqkv1_ref, *rest
+    where_ref, w_ref, gain_ref, dgain_two_ref, x_ref, h_t_ref, dx1_ref, dqkv0_ref, dqkv1_ref, *rest
 ):
-    gx_ref, send_ref, keep_ref = rest[handed : handed + 3]
+    gx_ref, send_ref, keep_ref, zero_ref = rest[-11:-7]
     dw_ref, dgain_ref, qs_ref, ks_ref, vs_ref, gs_ref, stage_ref = rest[-7:]
+    zero_ref[...] = jnp.zeros_like(zero_ref)
     dw = jnp.zeros((D, QKV), F32)
     dgain = jnp.zeros((D, 1), F32)
     for seq, dqkv_ref in enumerate((dqkv0_ref, dqkv1_ref)):
@@ -532,25 +529,21 @@
     lax.fori_loop(0, CHIPS, spread, 0)
 
 
-def qkv_bwd(args, handed):
-    handed = list(handed)
-    count = len(handed)
-    hbm = pl.BlockSpec(memory_space=pl.ANY)
+def qkv_bwd(args, after):
     seqs = args[4].shape[0]
     vmem = pl.BlockSpec(memory_space=pltpu.VMEM)
     return pl.pallas_call(
-        functools.partial(qkv_bwd_kernel, count),
+        qkv_bwd_kernel,
         in_specs=[pl.BlockSpec(memory_space=pltpu.SMEM)]
         + [vmem] * (len(args) - 1)
-        + [hbm] * count,
-        out_specs=[vmem] * 3 + [hbm] * count,
+        + [pl.BlockSpec(memory_space=pl.ANY)] * len(after),
+        out_specs=[vmem] * 4,
         out_shape=[
             jax.ShapeDtypeStruct((seqs, D, SEQ), F32),
             jax.ShapeDtypeStruct((CHIPS, ROWS_Q, 128), BF16),
             jax.ShapeDtypeStruct((CHIPS, ROWS_Q, 128), BF16),
-        ]
-        + [jax.ShapeDtypeStruct(v.shape, v.dtype) for v in handed],
-        input_output_aliases={len(args) + k: 3 + k for k in range(count)},
+            jax.ShapeDtypeStruct((8, 128), F32),
+        ],
         scratch_shapes=[
             pltpu.VMEM((D, QKV), F32),
             pltpu.VMEM((2 * D, 1), F32),
@@ -563,7 +556,7 @@
         compiler_params=pltpu.CompilerParams(vmem_limit_bytes=63 * 2**20),
         cost_estimate=pl.CostEstimate(flops=8 * 10**9, bytes_accessed=12 * 10**6, transcendentals=0),
         name="qkv_bwd",
-    )(*args, *handed)
+    )(*args, *after)
 
 
 def pairs(axis, step):
@@ -592,16 +585,22 @@
     return total
 
 
+def both(keep, got, place, zero):
+    rows = keep.shape[1]
+    keep = keep.reshape(4, 4, 4, rows, 128)[place]
+    got = got.reshape(4, 4, 4, rows, 128)[place]
+    return keep.astype(F32) + got.astype(F32) + zero[0, 0]
+
+
 def ring_far(far, axis):
-    cut = far.shape[0] // 2
-    return hop(far[:cut], axis, 1).astype(F32), hop(far[cut:], axis, 3).astype(F32)
-
-
-def ring_near(near, got, axis):
-    cut = near.shape[1] // 2
-    ahead = jnp.concatenate([near[0][:cut] + got[0], near[0][cut:]]).astype(BF16)
-    behind = jnp.concatenate([near[1][:cut], near[1][cut:] + got[1]]).astype(BF16)
-    return hop(ahead, axis, 1).astype(F32) + hop(behind, axis, 3).astype(F32)
+    return hop(far[:2], axis, 1).astype(F32), hop(far[2:], axis, 3).astype(F32)
+
+
+def ring_near(keep, got, arrived, zero):
+    ahead, behind = both(keep, got, 1, zero), both(keep, got, 3, zero)
+    ahead = jnp.concatenate([ahead[:2] + arrived[0], ahead[2:]])
+    behind = jnp.concatenate([behind[:2], behind[2:] + arrived[1]])
+    return ahead.astype(BF16), behind.astype(BF16)
 
 
 def on_device(
@@ -643,25 +642,20 @@
     got_g = hop(send_g, "c", 1)
     got_b = hop(send_b, "c", 1)
     args = [cos_t, sin_t, q_t, k_t, v_t, p, o_t, do_t]
-    dqkv0, keep_g, keep_b = attn_bwd(0, args, [keep_g, keep_b])
-
-    def halves(keep, got, rows):
-        v = (keep.astype(F32) + got.astype(F32)).reshape(4, 4, 4, rows, 128)
-        return v[2].astype(BF16), jnp.stack([v[1], v[3]]), v[0]
-
-    far_g, near_g, own_g = halves(keep_g, got_g, ROWS_G)
-    far_b, near_b, own_b = halves(keep_b, got_b, ROWS_B)
-    got_g = ring_far(far_g, "z")
-    got_b = ring_far(far_b, "y")
-    dqkv1, near_g, near_b = attn_bwd(1, args, [near_g, near_b])
-    sum_g = ring_near(near_g, got_g, "z")
-    sum_b = ring_near(near_b, got_b, "y")
-    gx_t, send_q, keep_q, own_g, own_b = qkv_bwd(
-        [where, wqkv, gain, dgain_two, x_t, h_t, dx1, dqkv0, dqkv1], [own_g, own_b]
+    dqkv0, zero = attn_bwd(0, args, [])
+    far_g = both(keep_g, got_g, 2, zero).astype(BF16)
+    far_b = both(keep_b, got_b, 2, zero).astype(BF16)
+    dqkv1, zero = attn_bwd(1, args, [far_g, far_b])
+    near_g = ring_near(keep_g, got_g, ring_far(far_g, "z"), zero)
+    near_b = ring_near(keep_b, got_b, ring_far(far_b, "y"), zero)
+    gx_t, send_q, keep_q, zero = qkv_bwd(
+        [where, wqkv, gain, dgain_two, x_t, h_t, dx1, dqkv0, dqkv1], near_g + near_b
     )
     got_q = hop(send_q, "c", 1)
-    sum_g = sum_g + own_g
-    sum_b = sum_b + own_b
+    sum_g = both(keep_g, got_g, 0, zero)
+    sum_g = sum_g + hop(near_g[0], "z", 1).astype(F32) + hop(near_g[1], "z", 3).astype(F32)
+    sum_b = both(keep_b, got_b, 0, zero)
+    sum_b = sum_b + hop(near_b[0], "y", 1).astype(F32) + hop(near_b[1], "y", 3).astype(F32)
     sum_q = (keep_q.astype(F32) + got_q.astype(F32)).reshape(4, 4, 4, ROWS_Q, 128)
     sum_q = sum_near(sum_q, "z")
     sum_b = sum_near(sum_b, "z")

time: 264 us -> 256 us (0.970)
  waiting for transfers between devices: 73.7 us -> 62.3 us
  other arithmetic: 20.1 us -> 24 us
    ppermute x23, waiting for transfers between devices: 31.4 us -> 20 us  [hop(): return lax.ppermute(v, 'dp', pairs(axis, step))]
    another operation x15 -> x11, other arithmetic: 12.8 us -> 2.36 us
    add x1 -> x5, other arithmetic: 1.34 us -> 9.47 us  [the longest x4 8.22 us: both(): return keep.astype(F32) + got.astype(F32) + zero[0, 0]]
    convert_element_type x0 -> x2, other arithmetic: none -> 4.61 us  [the longest x1 2.72 us: on_device(): far_b = both(keep_b, got_b, 2, zero).astype(BF16)]
  transfers between devices with their start and end apart: 25 -> 25, of which waited for: 11 -> 12; matrix products, arithmetic and copies ran while one was open for 10% -> 11% of each run, Pallas kernels for 21% -> 21%
where the time goes in v1:
time: 256 us; the launch traced here: 255 us
  Pallas kernels  97.2 us (38%)
  waiting for transfers between devices  62.3 us (24%)
  starting transfers between devices  37.6 us (15%)
  other arithmetic  24 us (9%)
  local copies, waits for them, and re-layouts  19 us (7%)
  between operations  14.5 us (6%)
    pallas_call x1, Pallas kernels, ffn(): pl.pallas_call(ffn_kernel, in_specs=[pl.BlockSpec(memory_space=pltpu.SMEM...  41.1 us
    ppermute x23, starting transfers between devices, hop(): return lax.ppermute(v, 'dp', pairs(axis, step))  26 us
    pallas_call x1, Pallas kernels, attn_fwd(): pl.pallas_call(attn_fwd_kernel, grid=(seqs,), in_specs=[whole_spec((2 * C...  22.8 us
    all_gather x1, waiting for transfers between devices, on_device(): all_f = lax.all_gather(pack_f, 'dp', axis=0, tiled=False)  21.6 us
    all_to_all x1, waiting for transfers between devices, on_device(): lax.all_to_all(jnp.broadcast_to(pack_q[None], (2 * CHIPS, ROWS_Q, 128)),...  20.8 us
    ppermute x23, waiting for transfers between devices, hop(): return lax.ppermute(v, 'dp', pairs(axis, step))  20 us
    pallas_call x2, Pallas kernels, attn_bwd(): pl.pallas_call(attn_bwd_kernel, grid=(1,), in_specs=[seq_spec((32, SEQ),...  19.8 us
    pallas_call x1, Pallas kernels, qkv_bwd(): pl.pallas_call(qkv_bwd_kernel, in_specs=[pl.BlockSpec(memory_space=pltpu....  12 us
  transfers between devices with their start and end apart: 25, of which 12 were waited for; matrix products, arithmetic and copies ran while one was open for 11% of the time, Pallas kernels for 21%

profile of v1, /device:TPU:0, one launch (start us, length us, event | category | flops | bytes accessed | tf_op | source)
XLA Modules:
  0.0 254.6 jit_solution(14039949400531323239)
XLA Ops:
  11.0 0.8 reshape.251
  13.0 1.3 pad_maximum_fusion.6.wgu
  14.4 1.4 pack.1
  15.8 2.1 broadcast_in_dim.2
  17.9 11.6 %all-to-all-start = ((bf16[128,48,128]{2,1,0:T(8,128)(2,1)}), bf16[128,48,128]{2,1,0:T(8,128)(2,1)}, u32[]{:S(2)}, u32[]{:S(2)}) async-start(bf16[128,48,128]{2,1,0:T(8,128)(2,1)} %broadcast_in_dim.2), calls=%async_computation | async-start | bytes 3145728 | tf_op jit(solution)/shard_map/all_to_all | solution.py:625
  30.8 1.2 reduce_window_sum.34.docc_ref
  32.6 1.2 multiply_sine_fusion
  33.8 20.8 %all-to-all-done.pack_ref = bf16[128,48,128]{2,1,0:T(8,128)(2,1)} async-done(((bf16[128,48,128]{2,1,0:T(8,128)(2,1)}), bf16[128,48,128]{2,1,0:T(8,128)(2,1)}, u32[]{:S(2)}, u32[]{:S(2)}) %all-to-all-start) | async-done | bytes 1572896 | tf_op jit(solution)/shard_map/all_to_all | solution.py:625
  54.6 22.8 %attn_fwd.1 = (bf16[576,960]{1,0:T(8,128)(2,1)}, f32[1152,1]{1,0:T(8,128)}, bf16[2,576,512]{2,1,0:T(8,128)(2,1)}, bf16[2,576,512]{2,1,0:T(8,128)(2,1)}, bf16[2,1...) custom-call(bf16[128,48,128]{2,1,0:T(8,128)(2,1)} %all-to-all-done.p, ...), custom_call_target="tpu_custom_call" | custom-call | flops 8000000000 | bytes 20000000 | tf_op jit(solution)/shard_map/attn_fwd/pallas_call | solution.py:221
  77.4 21.6 %all-gather.3.cloned.1.call-done = bf16[26624,128]{1,0:T(8,128)(2,1)} async-done(((bf16[208,128]{1,0:T(8,128)(2,1)}), bf16[26624,128]{1,0:T(8,128)(2,1)}) %all-gather.3.cloned.1.call-update) | async-done | bytes 6815760 | tf_op jit(solution)/shard_map/all_gather | solution.py:624
  98.9 41.1 %ffn.1 = (bf16[2,576,512]{2,1,0:T(8,128)(2,1)}, f32[2,576,512]{2,1,0:T(8,128)}, bf16[2,576,512]{2,1,0:T(8,128)(2,1)}, f32[576,1]{1,0:T(8,128)}, bf16[64,96,128]{...) custom-call(s32[4]{0:T(128)} %pad_add_fusion.where_ref, ...), custom_call_target="tpu_custom_call" | custom-call | flops 24999999488 | bytes 30000000 | tf_op jit(solution)/shard_map/ffn/pallas_call | solution.py:372
  140.6 9.9 %attn_bwd.2 = (bf16[960,512]{1,0:T(8,128)(2,1)}, f32[8,128]{1,0:T(8,128)}) custom-call(f32[2,32,512]{2,1,0:T(8,128)} %get-tuple-element.93.cos_ref, f32[2,32,512]{2,1,0:T(8,128)} %get-tuple-element.92.sin_ref, bf16[2,576,512]{2,1,0:T(8,128)(2,1)} %get-tuple-element.45.q_t_ref, bf16[2,192,512]{2,1,0:T(8,128)(2,1)} %get-tuple-element.46.k_t_ref, ...), custom_call_target="tpu_custom_call" | custom-call | flops 8000000000 | bytes 8000000 | tf_op jit(solution)/shard_map/attn_bwd/pallas_call | solution.py:456
  150.5 1.2 slice.295
  151.7 1.9 add_convert_fusion.1
  153.7 3.2 %collective-permute-start.3 = (bf16[2,4,96,128]{3,2,1,0:T(8,128)(2,1)S(1)}, bf16[2,4,96,128]{3,2,1,0:T(8,128)(2,1)S(1)}, u32[]{:S(2)}, u32[]{:S(2)}) collective-permute-start(bf16[2,4,96,128]{3,2,1,0:T(8,128)(2,1)S(1)} %bitcast.106), channel_id=1, source_target_pairs={{0,6},{1,7},{2,0},{3,1},{4,2},{5,3},{6,4},{7,5},{8,14},{9,15},{10,... | collective-permute-start | bytes 589832 | tf_op jit(solution)/shard_map/ppermute | solution.py:576
  156.9 2.7 %add_convert_fusion = bf16[16,112,128]{2,1,0:T(8,128)(2,1)} fusion(bf16[64,112,128]{2,1,0:T(8,128)(2,1)} %collective-permute-done.1, f32[]{:T(128)} %bitcast.12, bf16[64,112,128]{2,1,0:T(8,128)(2,1)} %get-tuple-element.54), kind=kLoop, calls=%fused_computation.9 | loop fusion | flops 1146880 | bytes 1376260 | tf_op jit(solution)/shard_map/convert_element_type | solution.py:647
  159.6 9.9 %attn_bwd.3 = (bf16[960,512]{1,0:T(8,128)(2,1)}, f32[8,128]{1,0:T(8,128)}) custom-call(f32[2,32,512]{2,1,0:T(8,128)} %get-tuple-element.93.cos_ref, f32[2,32,512]{2,1,0:T(8,128)} %get-tuple-element.92.sin_ref, bf16[2,576,512]{2,1,0:T(8,128)(2,1)} %get-tuple-element.45.q_t_ref, bf16[2,192,512]{2,1,0:T(8,128)(2,1)} %get-tuple-element.46.k_t_ref, ...), custom_call_target="tpu_custom_call" | custom-call | flops 8000000000 | bytes 8000000 | tf_op jit(solution)/shard_map/attn_bwd/pallas_call | solution.py:456
  169.5 1.2 slice.300
  170.7 2.4 add_add_fusion.4
  173.2 2.1 add_add_fusion.1
  175.4 0.8 copy-done
  176.6 3.0 %collective-permute-start.5 = (bf16[2,4,112,128]{3,2,1,0:T(8,128)(2,1)S(1)}, bf16[2,4,112,128]{3,2,1,0:T(8,128)(2,1)S(1)}, u32[]{:S(2)}, u32[]{:S(2)}) collective-permute-start(bf16[2,4,112,128]{3,2,1,0:T(8,128)(2,1)S(1)} %bitcast.101), channel_id=1, source_target_pairs={{0,24},{1,25},{2,26},{3,27},{4,28},{5,29},{6,30},{7,31},{8,0},{9,1... | collective-permute-start | bytes 688136 | tf_op jit(solution)/shard_map/ppermute | solution.py:576
  179.6 1.0 add_convert_fusion.5
  181.5 0.8 pad_maximum_fusion.5.rest_1_
  182.3 3.2 %collective-permute-start.7 = (bf16[4,4,96,128]{3,2,1,0:T(8,128)(2,1)}, bf16[4,4,96,128]{3,2,1,0:T(8,128)(2,1)}, u32[]{:S(2)}, u32[]{:S(2)}) collective-permute-start(bf16[4,4,96,128]{3,2,1,0:T(8,128)(2,1)} %pad_maximum_fusion.5.rest_1_), channel_id=1, source_target_pairs={{0,6},{1,7},{2,0},{3,1},{4,2},{5,3},{6,4},{7,5},{8,14},{9,15},{10,... | collective-permute-start | bytes 1179656 | tf_op jit(solution)/shard_map/ppermute | solution.py:576
  185.6 0.8 pad_maximum_fusion.2.rest_2_
  186.5 0.8 pad_maximum_fusion.3.rest_3_
  187.3 3.2 %collective-permute-start.16 = (bf16[4,4,112,128]{3,2,1,0:T(8,128)(2,1)}, bf16[4,4,112,128]{3,2,1,0:T(8,128)(2,1)S(1)}, u32[]{:S(2)}, u32[]{:S(2)}) collective-permute-start(bf16[4,4,112,128]{3,2,1,0:T(8,128)(2,1)} %pad_maximum_fusion.3.rest_3_), channel_id=1, source_target_pairs={{0,24},{1,25},{2,26},{3,27},{4,28},{5,29},{6,30},{7,31},{8,0},{9,1... | collective-permute-start | bytes 1376264 | tf_op jit(solution)/shard_map/ppermute | solution.py:576
  190.6 12.0 %qkv_bwd.1 = (f32[2,576,512]{2,1,0:T(8,128)}, bf16[64,48,128]{2,1,0:T(8,128)(2,1)}, bf16[64,48,128]{2,1,0:T(8,128)(2,1)}, f32[8,128]{1,0:T(8,128)}) custom-call(s32[4]{0:T(128)} %pad_add_fusion.where_ref, bf16[576,960]{1,0:T(8,128)(2,1)} %get-tuple-element.41.w_ref, f32[1152,1]{1,0:T(8,128)} %get-tuple-element.39.gain_ref, ...), custom_call_target="tpu_custom_call" | custom-call | flops 8000000000 | bytes 12000000 | tf_op jit(solution)/shard_map/qkv_bwd/pallas_call | solution.py:535
  202.6 1.2 slice.333
  203.8 1.9 add_add_fusion
  205.7 1.9 add_add_fusion.3
  207.6 1.3 convert_add_fusion.2
  209.1 0.9 copy-done.3
  210.4 0.8 collective-permute-start.9
  211.2 1.2 collective-permute-start.10
  212.4 4.2 %collective-permute-start.17 = (bf16[4,112,128]{2,1,0:T(8,128)(2,1)S(1)}, bf16[4,112,128]{2,1,0:T(8,128)(2,1)S(1)}, u32[]{:S(2)}, u32[]{:S(2)}) collective-permute-start(bf16[4,112,128]{2,1,0:T(8,128)(2,1)S(1)} %get-tuple-element.76), channel_id=1, source_target_pairs={{0,4},{1,5},{2,6},{3,7},{4,0},{5,1},{6,2},{7,3},{8,12},{9,13},{10,... | collective-permute-start | bytes 344072 | tf_op jit(solution)/shard_map/ppermute | solution.py:576
  216.7 1.3 collective-permute-done.11
  218.8 0.9 collective-permute-done.9
  219.7 4.2 %collective-permute-done.10 = bf16[4,4,48,128]{3,2,1,0:T(8,128)(2,1)S(1)} collective-permute-done((bf16[4,4,48,128]{3,2,1,0:T(8,128)(2,1)S(1)}, bf16[4,4,48,128]{3,2,1,0:T(8,128)(2,1)S(1)}, u32[]{:S(2)}, u32[]{:S(2)}) %collective-permute-start.10) | collective-permute-done | bytes 196640 | tf_op jit(solution)/shard_map/ppermute | solution.py:576
  224.2 1.4 collective-permute-start.14
  226.8 1.6 collective-permute-done.18
  228.5 4.0 %collective-permute-done.12 = bf16[4,144,128]{2,1,0:T(8,128)(2,1)S(1)} collective-permute-done((bf16[4,144,128]{2,1,0:T(8,128)(2,1)S(1)}, bf16[4,144,128]{2,1,0:T(8,128)(2,1)S(1)}, u32[]{:S(2)}, u32[]{:S(2)}) %collective-permute-start.12) | collective-permute-done | bytes 147488 | tf_op jit(solution)/shard_map/ppermute | solution.py:576
  232.5 2.0 collective-permute-done.13
  234.6 1.7 collective-permute-start.20
  236.4 1.3 collective-permute-start.22
  238.4 2.7 %collective-permute-done.20 = bf16[256,128]{1,0:T(8,128)(2,1)S(1)} collective-permute-done((bf16[256,128]{1,0:T(8,128)(2,1)S(1)}, bf16[256,128]{1,0:T(8,128)(2,1)S(1)}, u32[]{:S(2)}, u32[]{:S(2)}) %collective-permute-start.20) | collective-permute-done | bytes 65568 | tf_op jit(solution)/shard_map/ppermute | solution.py:576
  241.1 2.0 collective-permute-done.21
  (99 shorter events, 17.3 us)
Async XLA Ops:
  7.2 91.8 %all-gather.3.cloned.1.call-start = ((), (), s32[]{:S(2)}) async-start(), calls=%async_computation.1 | async-start | bytes 6868992 | tf_op jit(solution)/shard_map/all_gather | solution.py:624
  17.9 11.7 %copy-start.4 = (s32[2,512]{1,0:T(2,128)S(1)}, s32[2,512]{1,0:T(2,128)}, u32[]{:S(2)}) copy-start(s32[2,512]{1,0:T(2,128)} %param.12) | copy-start | bytes 12292
  17.9 36.7 %all-to-all-start = ((bf16[128,48,128]{2,1,0:T(8,128)(2,1)}), bf16[128,48,128]{2,1,0:T(8,128)(2,1)}, u32[]{:S(2)}, u32[]{:S(2)}) async-start(bf16[128,48,128]{2,1,0:T(8,128)(2,1)} %broadcast_in_dim.2), calls=%async_computation | async-start | bytes 3145728 | tf_op jit(solution)/shard_map/all_to_all | solution.py:625
  30.8 23.8 %copy-start.5 = (s32[2,4,128]{2,1,0:T(4,128)}, s32[2,4,128]{2,1,0:T(4,128)S(1)}, u32[]{:S(2)}) copy-start(s32[2,4,128]{2,1,0:T(4,128)S(1)} %broadcast_add_fusion) | copy-start | bytes 12292
  140.1 11.6 %collective-permute-start = (bf16[64,96,128]{2,1,0:T(8,128)(2,1)}, bf16[64,96,128]{2,1,0:T(8,128)(2,1)}, u32[]{:S(2)}, u32[]{:S(2)}) collective-permute-start(bf16[64,96,128]{2,1,0:T(8,128)(2,1)} %get-tuple-element.52), channel_id=1, source_target_pairs={{0,1},{1,0},{2,3},{3,2},{4,5},{5,4},{6,7},{7,6},{8,9},{9,8},{10,11... | collective-permute-start | bytes 4718600 | tf_op jit(solution)/shard_map/ppermute | solution.py:576
  140.3 16.6 %collective-permute-start.1 = (bf16[64,112,128]{2,1,0:T(8,128)(2,1)}, bf16[64,112,128]{2,1,0:T(8,128)(2,1)}, u32[]{:S(2)}, u32[]{:S(2)}) collective-permute-start(bf16[64,112,128]{2,1,0:T(8,128)(2,1)} %get-tuple-element.55), channel_id=1, source_target_pairs={{0,1},{1,0},{2,3},{3,2},{4,5},{5,4},{6,7},{7,6},{8,9},{9,8},{10,11... | collective-permute-start | bytes 5505032 | tf_op jit(solution)/shard_map/ppermute | solution.py:576
  153.6 6.1 %copy-start.2 = (bf16[16,96,128]{2,1,0:T(8,128)(2,1)}, bf16[16,96,128]{2,1,0:T(8,128)(2,1)S(1)}, u32[]{:S(2)}) copy-start(bf16[16,96,128]{2,1,0:T(8,128)(2,1)S(1)} %add_convert_fusion.1) | copy-start | bytes 1179652
  153.6 26.0 %collective-permute-start.2 = (bf16[2,4,96,128]{3,2,1,0:T(8,128)(2,1)S(1)}, bf16[2,4,96,128]{3,2,1,0:T(8,128)(2,1)}, u32[]{:S(2)}, u32[]{:S(2)}) collective-permute-start(bf16[2,4,96,128]{3,2,1,0:T(8,128)(2,1)S(1)} %bitcast.107), channel_id=1, source_target_pairs={{0,2},{1,3},{2,4},{3,5},{4,6},{5,7},{6,0},{7,1},{8,10},{9,11},{10,... | collective-permute-start | bytes 589832 | tf_op jit(solution)/shard_map/ppermute | solution.py:576
  153.7 27.7 %collective-permute-start.3 = (bf16[2,4,96,128]{3,2,1,0:T(8,128)(2,1)S(1)}, bf16[2,4,96,128]{3,2,1,0:T(8,128)(2,1)S(1)}, u32[]{:S(2)}, u32[]{:S(2)}) collective-permute-start(bf16[2,4,96,128]{3,2,1,0:T(8,128)(2,1)S(1)} %bitcast.106), channel_id=1, source_target_pairs={{0,6},{1,7},{2,0},{3,1},{4,2},{5,3},{6,4},{7,5},{8,14},{9,15},{10,... | collective-permute-start | bytes 589832 | tf_op jit(solution)/shard_map/ppermute | solution.py:576
  170.7 2.5 copy-start.1
  175.3 1.0 copy-start
  176.3 9.3 %collective-permute-start.4 = (bf16[2,4,112,128]{3,2,1,0:T(8,128)(2,1)S(1)}, bf16[2,4,112,128]{3,2,1,0:T(8,128)(2,1)S(1)}, u32[]{:S(2)}, u32[]{:S(2)}) collective-permute-start(bf16[2,4,112,128]{3,2,1,0:T(8,128)(2,1)S(1)} %bitcast.102), channel_id=1, source_target_pairs={{0,8},{1,9},{2,10},{3,11},{4,12},{5,13},{6,14},{7,15},{8,16},{9,17... | collective-permute-start | bytes 688136 | tf_op jit(solution)/shard_map/ppermute | solution.py:576
  176.6 9.9 %collective-permute-start.5 = (bf16[2,4,112,128]{3,2,1,0:T(8,128)(2,1)S(1)}, bf16[2,4,112,128]{3,2,1,0:T(8,128)(2,1)S(1)}, u32[]{:S(2)}, u32[]{:S(2)}) collective-permute-start(bf16[2,4,112,128]{3,2,1,0:T(8,128)(2,1)S(1)} %bitcast.101), channel_id=1, source_target_pairs={{0,24},{1,25},{2,26},{3,27},{4,28},{5,29},{6,30},{7,31},{8,0},{9,1... | collective-permute-start | bytes 688136 | tf_op jit(solution)/shard_map/ppermute | solution.py:576
  181.4 26.2 %collective-permute-start.6 = (bf16[4,4,96,128]{3,2,1,0:T(8,128)(2,1)}, bf16[4,4,96,128]{3,2,1,0:T(8,128)(2,1)}, u32[]{:S(2)}, u32[]{:S(2)}) collective-permute-start(bf16[4,4,96,128]{3,2,1,0:T(8,128)(2,1)} %pad_maximum_fusion.4.rest_0_), channel_id=1, source_target_pairs={{0,2},{1,3},{2,4},{3,5},{4,6},{5,7},{6,0},{7,1},{8,10},{9,11},{10,... | collective-permute-start | bytes 1179656 | tf_op jit(solution)/shard_map/ppermute | solution.py:576
  182.3 25.3 %collective-permute-start.7 = (bf16[4,4,96,128]{3,2,1,0:T(8,128)(2,1)}, bf16[4,4,96,128]{3,2,1,0:T(8,128)(2,1)}, u32[]{:S(2)}, u32[]{:S(2)}) collective-permute-start(bf16[4,4,96,128]{3,2,1,0:T(8,128)(2,1)} %pad_maximum_fusion.5.rest_1_), channel_id=1, source_target_pairs={{0,6},{1,7},{2,0},{3,1},{4,2},{5,3},{6,4},{7,5},{8,14},{9,15},{10,... | collective-permute-start | bytes 1179656 | tf_op jit(solution)/shard_map/ppermute | solution.py:576
  186.5 22.4 %collective-permute-start.15 = (bf16[4,4,112,128]{3,2,1,0:T(8,128)(2,1)}, bf16[4,4,112,128]{3,2,1,0:T(8,128)(2,1)S(1)}, u32[]{:S(2)}, u32[]{:S(2)}) collective-permute-start(bf16[4,4,112,128]{3,2,1,0:T(8,128)(2,1)} %pad_maximum_fusion.2.rest_2_), channel_id=1, source_target_pairs={{0,8},{1,9},{2,10},{3,11},{4,12},{5,13},{6,14},{7,15},{8,16},{9,17... | collective-permute-start | bytes 1376264 | tf_op jit(solution)/shard_map/ppermute | solution.py:576
  187.3 21.6 %collective-permute-start.16 = (bf16[4,4,112,128]{3,2,1,0:T(8,128)(2,1)}, bf16[4,4,112,128]{3,2,1,0:T(8,128)(2,1)S(1)}, u32[]{:S(2)}, u32[]{:S(2)}) collective-permute-start(bf16[4,4,112,128]{3,2,1,0:T(8,128)(2,1)} %pad_maximum_fusion.3.rest_3_), channel_id=1, source_target_pairs={{0,24},{1,25},{2,26},{3,27},{4,28},{5,29},{6,30},{7,31},{8,0},{9,1... | collective-permute-start | bytes 1376264 | tf_op jit(solution)/shard_map/ppermute | solution.py:576
  203.8 5.3 %collective-permute-start.8 = (bf16[64,48,128]{2,1,0:T(8,128)(2,1)}, bf16[64,48,128]{2,1,0:T(8,128)(2,1)S(1)}, u32[]{:S(2)}, u32[]{:S(2)}) collective-permute-start(bf16[64,48,128]{2,1,0:T(8,128)(2,1)} %get-tuple-element.61), channel_id=1, source_target_pairs={{0,1},{1,0},{2,3},{3,2},{4,5},{5,4},{6,7},{7,6},{8,9},{9,8},{10,11... | collective-permute-start | bytes 2359304 | tf_op jit(solution)/shard_map/ppermute | solution.py:576
  208.9 1.1 copy-start.3
  210.3 7.8 %collective-permute-start.11 = (bf16[4,4,48,128]{3,2,1,0:T(8,128)(2,1)S(1)}, bf16[4,4,48,128]{3,2,1,0:T(8,128)(2,1)S(1)}, u32[]{:S(2)}, u32[]{:S(2)}) collective-permute-start(bf16[4,4,48,128]{3,2,1,0:T(8,128)(2,1)S(1)} %bitcast.105), channel_id=1, source_target_pairs={{0,6},{1,7},{2,0},{3,1},{4,2},{5,3},{6,4},{7,5},{8,14},{9,15},{10,... | collective-permute-start | bytes 589832 | tf_op jit(solution)/shard_map/ppermute | solution.py:576
  210.4 9.3 %collective-permute-start.9 = (bf16[4,4,48,128]{3,2,1,0:T(8,128)(2,1)S(1)}, bf16[4,4,48,128]{3,2,1,0:T(8,128)(2,1)S(1)}, u32[]{:S(2)}, u32[]{:S(2)}) collective-permute-start(bf16[4,4,48,128]{3,2,1,0:T(8,128)(2,1)S(1)} %bitcast.104), channel_id=1, source_target_pairs={{0,4},{1,5},{2,6},{3,7},{4,0},{5,1},{6,2},{7,3},{8,12},{9,13},{10,... | collective-permute-start | bytes 589832 | tf_op jit(solution)/shard_map/ppermute | solution.py:576
  211.2 12.7 %collective-permute-start.10 = (bf16[4,4,48,128]{3,2,1,0:T(8,128)(2,1)S(1)}, bf16[4,4,48,128]{3,2,1,0:T(8,128)(2,1)S(1)}, u32[]{:S(2)}, u32[]{:S(2)}) collective-permute-start(bf16[4,4,48,128]{3,2,1,0:T(8,128)(2,1)S(1)} %bitcast.103), channel_id=1, source_target_pairs={{0,2},{1,3},{2,4},{3,5},{4,6},{5,7},{6,0},{7,1},{8,10},{9,11},{10,... | collective-permute-start | bytes 589832 | tf_op jit(solution)/shard_map/ppermute | solution.py:576
  212.4 14.0 %collective-permute-start.17 = (bf16[4,112,128]{2,1,0:T(8,128)(2,1)S(1)}, bf16[4,112,128]{2,1,0:T(8,128)(2,1)S(1)}, u32[]{:S(2)}, u32[]{:S(2)}) collective-permute-start(bf16[4,112,128]{2,1,0:T(8,128)(2,1)S(1)} %get-tuple-element.76), channel_id=1, source_target_pairs={{0,4},{1,5},{2,6},{3,7},{4,0},{5,1},{6,2},{7,3},{8,12},{9,13},{10,... | collective-permute-start | bytes 344072 | tf_op jit(solution)/shard_map/ppermute | solution.py:576
  216.6 10.2 %collective-permute-start.19 = (bf16[4,112,128]{2,1,0:T(8,128)(2,1)S(1)}, bf16[4,112,128]{2,1,0:T(8,128)(2,1)S(1)}, u32[]{:S(2)}, u32[]{:S(2)}) collective-permute-start(bf16[4,112,128]{2,1,0:T(8,128)(2,1)S(1)} %get-tuple-element.77), channel_id=1, source_target_pairs={{0,6},{1,7},{2,0},{3,1},{4,2},{5,3},{6,4},{7,5},{8,14},{9,15},{10,... | collective-permute-start | bytes 344072 | tf_op jit(solution)/shard_map/ppermute | solution.py:576
  218.0 10.3 %collective-permute-start.18 = (bf16[4,112,128]{2,1,0:T(8,128)(2,1)S(1)}, bf16[4,112,128]{2,1,0:T(8,128)(2,1)S(1)}, u32[]{:S(2)}, u32[]{:S(2)}) collective-permute-start(bf16[4,112,128]{2,1,0:T(8,128)(2,1)S(1)} %get-tuple-element.78), channel_id=1, source_target_pairs={{0,2},{1,3},{2,4},{3,5},{4,6},{5,7},{6,0},{7,1},{8,10},{9,11},{10,... | collective-permute-start | bytes 344072 | tf_op jit(solution)/shard_map/ppermute | solution.py:576
  224.2 8.3 %collective-permute-start.12 = (bf16[4,144,128]{2,1,0:T(8,128)(2,1)S(1)}, bf16[4,144,128]{2,1,0:T(8,128)(2,1)S(1)}, u32[]{:S(2)}, u32[]{:S(2)}) collective-permute-start(bf16[4,144,128]{2,1,0:T(8,128)(2,1)S(1)} %get-tuple-element.73), channel_id=1, source_target_pairs={{0,16},{1,17},{2,18},{3,19},{4,20},{5,21},{6,22},{7,23},{8,24},{9,... | collective-permute-start | bytes 442376 | tf_op jit(solution)/shard_map/ppermute | solution.py:576
  224.2 8.2 %collective-permute-start.14 = (bf16[4,144,128]{2,1,0:T(8,128)(2,1)S(1)}, bf16[4,144,128]{2,1,0:T(8,128)(2,1)S(1)}, u32[]{:S(2)}, u32[]{:S(2)}) collective-permute-start(bf16[4,144,128]{2,1,0:T(8,128)(2,1)S(1)} %get-tuple-element.74), channel_id=1, source_target_pairs={{0,24},{1,25},{2,26},{3,27},{4,28},{5,29},{6,30},{7,31},{8,0},{9,1... | collective-permute-start | bytes 442376 | tf_op jit(solution)/shard_map/ppermute | solution.py:576
  226.4 8.1 %collective-permute-start.13 = (bf16[4,144,128]{2,1,0:T(8,128)(2,1)S(1)}, bf16[4,144,128]{2,1,0:T(8,128)(2,1)S(1)}, u32[]{:S(2)}, u32[]{:S(2)}) collective-permute-start(bf16[4,144,128]{2,1,0:T(8,128)(2,1)S(1)} %get-tuple-element.75), channel_id=1, source_target_pairs={{0,8},{1,9},{2,10},{3,11},{4,12},{5,13},{6,14},{7,15},{8,16},{9,17... | collective-permute-start | bytes 442376 | tf_op jit(solution)/shard_map/ppermute | solution.py:576
  234.6 6.5 %collective-permute-start.20 = (bf16[256,128]{1,0:T(8,128)(2,1)S(1)}, bf16[256,128]{1,0:T(8,128)(2,1)S(1)}, u32[]{:S(2)}, u32[]{:S(2)}) collective-permute-start(bf16[256,128]{1,0:T(8,128)(2,1)S(1)} %get-tuple-element.83), channel_id=1, source_target_pairs={{0,64},{1,65},{2,66},{3,67},{4,68},{5,69},{6,70},{7,71},{8,72},{9,... | collective-permute-start | bytes 196616 | tf_op jit(solution)/shard_map/ppermute | solution.py:576
  236.4 4.8 %collective-permute-start.22 = (bf16[256,128]{1,0:T(8,128)(2,1)S(1)}, bf16[256,128]{1,0:T(8,128)(2,1)S(1)}, u32[]{:S(2)}, u32[]{:S(2)}) collective-permute-start(bf16[256,128]{1,0:T(8,128)(2,1)S(1)} %get-tuple-element.84), channel_id=1, source_target_pairs={{0,96},{1,97},{2,98},{3,99},{4,100},{5,101},{6,102},{7,103},{8,104... | collective-permute-start | bytes 196616 | tf_op jit(solution)/shard_map/ppermute | solution.py:576
  237.6 5.5 %collective-permute-start.21 = (bf16[256,128]{1,0:T(8,128)(2,1)S(1)}, bf16[256,128]{1,0:T(8,128)(2,1)S(1)}, u32[]{:S(2)}, u32[]{:S(2)}) collective-permute-start(bf16[256,128]{1,0:T(8,128)(2,1)S(1)} %get-tuple-element.85), channel_id=1, source_target_pairs={{0,32},{1,33},{2,34},{3,35},{4,36},{5,37},{6,38},{7,39},{8,40},{9,... | collective-permute-start | bytes 196616 | tf_op jit(solution)/shard_map/ppermute | solution.py:576
Sparse Core Ops, SparseCore 0:
  16.0 82.9 all-gather.2

commit v2 on v1

--- a/solution.py
+++ b/solution.py
@@ -476,7 +476,7 @@
             pltpu.VMEM((D + KVW, SEQ), F32),
             pltpu.VMEM((KV_HEADS, SEQ, HEAD), BF16),
         ],
-        compiler_params=pltpu.CompilerParams(vmem_limit_bytes=63 * 2**20),
+        compiler_params=pltpu.CompilerParams(vmem_limit_bytes=(63 if seq == 0 else 40) * 2**20),
         cost_estimate=pl.CostEstimate(flops=8 * 10**9, bytes_accessed=8 * 10**6, transcendentals=0),
         name="attn_bwd",
     )(*args, *after)
@@ -553,7 +553,7 @@
             pltpu.VMEM((2 * CHIPS, 128), F32),
             pltpu.VMEM((ROWS_Q, 128), F32),
         ],
-        compiler_params=pltpu.CompilerParams(vmem_limit_bytes=63 * 2**20),
+        compiler_params=pltpu.CompilerParams(vmem_limit_bytes=40 * 2**20),
         cost_estimate=pl.CostEstimate(flops=8 * 10**9, bytes_accessed=12 * 10**6, transcendentals=0),
         name="qkv_bwd",
     )(*args, *after)

time: 256 us -> 245 us (0.957)
  other arithmetic: 24 us -> 17.9 us
  Pallas kernels: 97.2 us -> 92.1 us
    pallas_call x1, Pallas kernels: 12 us -> 8.43 us  [qkv_bwd(): pl.pallas_call(qkv_bwd_kernel, in_specs=[pl.BlockSpec(memory_space=pltpu....]
  transfers between devices with their start and end apart: 25 -> 25, of which waited for: 12 -> 13; matrix products, arithmetic and copies ran while one was open for 11% -> 9% of each run, Pallas kernels for 21% -> 20%
where the time goes in v2:
time: 245 us; the launch traced here: 244 us
  Pallas kernels  92.1 us (38%)
  waiting for transfers between devices  63.7 us (26%)
  starting transfers between devices  38.8 us (16%)
  other arithmetic  17.9 us (7%)
  local copies, waits for them, and re-layouts  17.1 us (7%)
  between operations  14.7 us (6%)
    pallas_call x1, Pallas kernels, ffn(): pl.pallas_call(ffn_kernel, in_specs=[pl.BlockSpec(memory_space=pltpu.SMEM...  41.2 us
    ppermute x23, starting transfers between devices, hop(): return lax.ppermute(v, 'dp', pairs(axis, step))  27.2 us
    pallas_call x1, Pallas kernels, attn_fwd(): pl.pallas_call(attn_fwd_kernel, grid=(seqs,), in_specs=[whole_spec((2 * C...  22.8 us
    all_gather x1, waiting for transfers between devices, on_device(): all_f = lax.all_gather(pack_f, 'dp', axis=0, tiled=False)  21.6 us
    ppermute x23, waiting for transfers between devices, hop(): return lax.ppermute(v, 'dp', pairs(axis, step))  21.4 us
    all_to_all x1, waiting for transfers between devices, on_device(): lax.all_to_all(jnp.broadcast_to(pack_q[None], (2 * CHIPS, ROWS_Q, 128)),...  20.7 us
    pallas_call x2, Pallas kernels, attn_bwd(): pl.pallas_call(attn_bwd_kernel, grid=(1,), in_specs=[seq_spec((32, SEQ),...  18.3 us
    all_to_all x1, starting transfers between devices, on_device(): lax.all_to_all(jnp.broadcast_to(pack_q[None], (2 * CHIPS, ROWS_Q, 128)),...  11.6 us
  transfers between devices with their start and end apart: 25, of which 13 were waited for; matrix products, arithmetic and copies ran while one was open for 9% of the time, Pallas kernels for 20%

profile of v2, /device:TPU:0, one launch (start us, length us, event | category | flops | bytes accessed | tf_op | source)
XLA Modules:
  0.0 244.3 jit_solution(1432009265390424514)
XLA Ops:
  7.2 0.8 concatenate.49
  8.0 0.8 concatenate.50
  8.8 0.8 concatenate.46
  9.5 0.8 concatenate.47
  11.0 0.8 reshape.251
  13.0 1.3 pad_maximum_fusion.6.wgu
  14.4 1.4 pack.1
  15.8 2.1 broadcast_in_dim.2
  17.9 11.6 %all-to-all-start = ((bf16[128,48,128]{2,1,0:T(8,128)(2,1)}), bf16[128,48,128]{2,1,0:T(8,128)(2,1)}, u32[]{:S(2)}, u32[]{:S(2)}) async-start(bf16[128,48,128]{2,1,0:T(8,128)(2,1)} %broadcast_in_dim.2), calls=%async_computation | async-start | bytes 3145728 | tf_op jit(solution)/shard_map/all_to_all | solution.py:625
  30.8 1.2 reduce_window_sum.34.docc_ref
  32.6 1.3 multiply_sine_fusion
  33.9 20.7 %all-to-all-done.pack_ref = bf16[128,48,128]{2,1,0:T(8,128)(2,1)} async-done(((bf16[128,48,128]{2,1,0:T(8,128)(2,1)}), bf16[128,48,128]{2,1,0:T(8,128)(2,1)}, u32[]{:S(2)}, u32[]{:S(2)}) %all-to-all-start) | async-done | bytes 1572896 | tf_op jit(solution)/shard_map/all_to_all | solution.py:625
  54.6 22.8 %attn_fwd.1 = (bf16[576,960]{1,0:T(8,128)(2,1)}, f32[1152,1]{1,0:T(8,128)}, bf16[2,576,512]{2,1,0:T(8,128)(2,1)}, bf16[2,576,512]{2,1,0:T(8,128)(2,1)}, bf16[2,1...) custom-call(bf16[128,48,128]{2,1,0:T(8,128)(2,1)} %all-to-all-done.p, ...), custom_call_target="tpu_custom_call" | custom-call | flops 8000000000 | bytes 20000000 | tf_op jit(solution)/shard_map/attn_fwd/pallas_call | solution.py:221
  77.4 21.6 %all-gather.3.cloned.1.call-done = bf16[26624,128]{1,0:T(8,128)(2,1)} async-done(((bf16[208,128]{1,0:T(8,128)(2,1)}), bf16[26624,128]{1,0:T(8,128)(2,1)}) %all-gather.3.cloned.1.call-update) | async-done | bytes 6815760 | tf_op jit(solution)/shard_map/all_gather | solution.py:624
  98.9 41.2 %ffn.1 = (bf16[2,576,512]{2,1,0:T(8,128)(2,1)}, f32[2,576,512]{2,1,0:T(8,128)}, bf16[2,576,512]{2,1,0:T(8,128)(2,1)}, f32[576,1]{1,0:T(8,128)}, bf16[64,96,128]{...) custom-call(s32[4]{0:T(128)} %pad_add_fusion.where_ref, ...), custom_call_target="tpu_custom_call" | custom-call | flops 24999999488 | bytes 30000000 | tf_op jit(solution)/shard_map/ffn/pallas_call | solution.py:372
  140.6 9.9 %attn_bwd.2 = (bf16[960,512]{1,0:T(8,128)(2,1)}, f32[8,128]{1,0:T(8,128)}) custom-call(f32[2,32,512]{2,1,0:T(8,128)} %get-tuple-element.93.cos_ref, f32[2,32,512]{2,1,0:T(8,128)} %get-tuple-element.92.sin_ref, bf16[2,576,512]{2,1,0:T(8,128)(2,1)} %get-tuple-element.45.q_t_ref, bf16[2,192,512]{2,1,0:T(8,128)(2,1)} %get-tuple-element.46.k_t_ref, ...), custom_call_target="tpu_custom_call" | custom-call | flops 8000000000 | bytes 8000000 | tf_op jit(solution)/shard_map/attn_bwd/pallas_call | solution.py:456
  150.5 1.2 slice.295
  151.8 2.2 add_convert_fusion.1
  154.1 3.2 %collective-permute-start.3 = (bf16[2,4,96,128]{3,2,1,0:T(8,128)(2,1)S(1)}, bf16[2,4,96,128]{3,2,1,0:T(8,128)(2,1)S(1)}, u32[]{:S(2)}, u32[]{:S(2)}) collective-permute-start(bf16[2,4,96,128]{3,2,1,0:T(8,128)(2,1)S(1)} %bitcast.109), channel_id=1, source_target_pairs={{0,6},{1,7},{2,0},{3,1},{4,2},{5,3},{6,4},{7,5},{8,14},{9,15},{10,... | collective-permute-start | bytes 589832 | tf_op jit(solution)/shard_map/ppermute | solution.py:576
  157.3 2.0 add_convert_fusion
  159.3 1.3 copy-done.7
  160.6 8.4 %attn_bwd.3 = (bf16[960,512]{1,0:T(8,128)(2,1)S(1)}, f32[8,128]{1,0:T(8,128)S(1)}) custom-call(f32[2,32,512]{2,1,0:T(8,128)S(1)} %copy-done.1, f32[2,32,512]{2,1,0:T(8,128)S(1)} %copy-done, bf16[2,576,512]{2,1,0:T(8,128)(2,1)S(1)} %copy-done.5, bf16[2,192,512]{2,1,0:T(8,128)(2,1)S(1)} %copy-done.11, bf16[2,192,512]{2,1,0:T(8,128)(2,1)S(1)} %copy-done.12, ...), custom_call_target="tpu_custom_call" | custom-call | flops 8000000000 | bytes 8000000 | tf_op jit(solution)/shard_map/attn_bwd/pallas_call | solution.py:456
  169.5 2.1 add_add_fusion.4
  171.7 2.0 add_add_fusion.1
  174.2 3.0 %collective-permute-start.5 = (bf16[2,4,112,128]{3,2,1,0:T(8,128)(2,1)S(1)}, bf16[2,4,112,128]{3,2,1,0:T(8,128)(2,1)S(1)}, u32[]{:S(2)}, u32[]{:S(2)}) collective-permute-start(bf16[2,4,112,128]{3,2,1,0:T(8,128)(2,1)S(1)} %bitcast.104), channel_id=1, source_target_pairs={{0,24},{1,25},{2,26},{3,27},{4,28},{5,29},{6,30},{7,31},{8,0},{9,1... | collective-permute-start | bytes 688136 | tf_op jit(solution)/shard_map/ppermute | solution.py:576
  177.6 3.3 %collective-permute-start.7 = (bf16[4,4,96,128]{3,2,1,0:T(8,128)(2,1)S(1)}, bf16[4,4,96,128]{3,2,1,0:T(8,128)(2,1)S(1)}, u32[]{:S(2)}, u32[]{:S(2)}) collective-permute-start(bf16[4,4,96,128]{3,2,1,0:T(8,128)(2,1)S(1)} %pad_maximum_fusion.5.rest_1_), channel_id=1, source_target_pairs={{0,6},{1,7},{2,0},{3,1},{4,2},{5,3},{6,4},{7,5},{8,14},{9,15},{10,... | collective-permute-start | bytes 1179656 | tf_op jit(solution)/shard_map/ppermute | solution.py:576
  180.9 1.5 collective-permute-done.4
  182.7 3.5 %collective-permute-start.16 = (bf16[4,4,112,128]{3,2,1,0:T(8,128)(2,1)S(1)}, bf16[4,4,112,128]{3,2,1,0:T(8,128)(2,1)S(1)}, u32[]{:S(2)}, u32[]{:S(2)}) collective-permute-start(bf16[4,4,112,128]{3,2,1,0:T(8,128)(2,1)S(1)} %pad_maximum_fusion.3.rest_3_), channel_id=1, source_target_pairs={{0,24},{1,25},{2,26},{3,27},{4,28},{5,29},{6,30},{7,31},{8,0},{9,1... | collective-permute-start | bytes 1376264 | tf_op jit(solution)/shard_map/ppermute | solution.py:576
  186.3 8.4 %qkv_bwd.1 = (f32[2,576,512]{2,1,0:T(8,128)}, bf16[64,48,128]{2,1,0:T(8,128)(2,1)S(1)}, bf16[64,48,128]{2,1,0:T(8,128)(2,1)S(1)}, f32[8,128]{1,0:T(8,128)S(1)}) custom-call(s32[4]{0:T(128)S(1)} %copy-done.2, bf16[576,960]{1,0:T(8,128)(2,1)S(1)} %copy-done.9, f32[1152,1]{1,0:T(8,128)S(1)} %copy-done.13, f32[576,1]{1,0:T(8,128)S(1)} %copy-done.14, ...), custom_call_target="tpu_custom_call" | custom-call | flops 8000000000 | bytes 12000000 | tf_op jit(solution)/shard_map/qkv_bwd/pallas_call | solution.py:535
  195.2 1.8 add_add_fusion
  197.0 1.7 add_add_fusion.3
  199.7 0.9 collective-permute-start.9
  200.6 0.8 collective-permute-start.10
  201.5 4.2 %collective-permute-start.17 = (bf16[4,112,128]{2,1,0:T(8,128)(2,1)S(1)}, bf16[4,112,128]{2,1,0:T(8,128)(2,1)S(1)}, u32[]{:S(2)}, u32[]{:S(2)}) collective-permute-start(bf16[4,112,128]{2,1,0:T(8,128)(2,1)S(1)} %get-tuple-element.76), channel_id=1, source_target_pairs={{0,4},{1,5},{2,6},{3,7},{4,0},{5,1},{6,2},{7,3},{8,12},{9,13},{10,... | collective-permute-start | bytes 344072 | tf_op jit(solution)/shard_map/ppermute | solution.py:576
  206.0 1.1 collective-permute-done.11
  207.1 0.7 collective-permute-start.18
  207.8 1.2 collective-permute-done.9
  209.0 4.2 %collective-permute-done.10 = bf16[4,4,48,128]{3,2,1,0:T(8,128)(2,1)S(1)} collective-permute-done((bf16[4,4,48,128]{3,2,1,0:T(8,128)(2,1)S(1)}, bf16[4,4,48,128]{3,2,1,0:T(8,128)(2,1)S(1)}, u32[]{:S(2)}, u32[]{:S(2)}) %collective-permute-start.10) | collective-permute-done | bytes 196640 | tf_op jit(solution)/shard_map/ppermute | solution.py:576
  213.6 1.5 collective-permute-start.14
  215.9 1.6 collective-permute-done.18
  217.5 4.3 %collective-permute-done.12 = bf16[4,144,128]{2,1,0:T(8,128)(2,1)S(1)} collective-permute-done((bf16[4,144,128]{2,1,0:T(8,128)(2,1)S(1)}, bf16[4,144,128]{2,1,0:T(8,128)(2,1)S(1)}, u32[]{:S(2)}, u32[]{:S(2)}) %collective-permute-start.12) | collective-permute-done | bytes 147488 | tf_op jit(solution)/shard_map/ppermute | solution.py:576
  221.8 2.0 collective-permute-done.13
  224.0 2.2 collective-permute-start.20
  226.2 1.2 collective-permute-start.22
  227.4 0.8 collective-permute-start.21
  228.2 2.2 collective-permute-done.20
  230.5 2.4 collective-permute-done.21
  235.4 0.7 reshape.265
  (125 shorter events, 13.1 us)
Async XLA Ops:
  7.2 91.8 %all-gather.3.cloned.1.call-start = ((), (), s32[]{:S(2)}) async-start(), calls=%async_computation.1 | async-start | bytes 6868992 | tf_op jit(solution)/shard_map/all_gather | solution.py:624
  17.9 11.7 %copy-start.17 = (s32[2,512]{1,0:T(2,128)S(1)}, s32[2,512]{1,0:T(2,128)}, u32[]{:S(2)}) copy-start(s32[2,512]{1,0:T(2,128)} %param.12) | copy-start | bytes 12292
  17.9 36.7 %all-to-all-start = ((bf16[128,48,128]{2,1,0:T(8,128)(2,1)}), bf16[128,48,128]{2,1,0:T(8,128)(2,1)}, u32[]{:S(2)}, u32[]{:S(2)}) async-start(bf16[128,48,128]{2,1,0:T(8,128)(2,1)} %broadcast_in_dim.2), calls=%async_computation | async-start | bytes 3145728 | tf_op jit(solution)/shard_map/all_to_all | solution.py:625
  30.8 23.8 %copy-start.18 = (s32[2,4,128]{2,1,0:T(4,128)}, s32[2,4,128]{2,1,0:T(4,128)S(1)}, u32[]{:S(2)}) copy-start(s32[2,4,128]{2,1,0:T(4,128)S(1)} %broadcast_add_fusion) | copy-start | bytes 12292
  140.1 11.7 %collective-permute-start = (bf16[64,96,128]{2,1,0:T(8,128)(2,1)}, bf16[64,96,128]{2,1,0:T(8,128)(2,1)}, u32[]{:S(2)}, u32[]{:S(2)}) collective-permute-start(bf16[64,96,128]{2,1,0:T(8,128)(2,1)} %get-tuple-element.52), channel_id=1, source_target_pairs={{0,1},{1,0},{2,3},{3,2},{4,5},{5,4},{6,7},{7,6},{8,9},{9,8},{10,11... | collective-permute-start | bytes 4718600 | tf_op jit(solution)/shard_map/ppermute | solution.py:576
  140.4 17.0 %collective-permute-start.1 = (bf16[64,112,128]{2,1,0:T(8,128)(2,1)}, bf16[64,112,128]{2,1,0:T(8,128)(2,1)}, u32[]{:S(2)}, u32[]{:S(2)}) collective-permute-start(bf16[64,112,128]{2,1,0:T(8,128)(2,1)} %get-tuple-element.55), channel_id=1, source_target_pairs={{0,1},{1,0},{2,3},{3,2},{4,5},{5,4},{6,7},{7,6},{8,9},{9,8},{10,11... | collective-permute-start | bytes 5505032 | tf_op jit(solution)/shard_map/ppermute | solution.py:576
  140.6 18.7 %copy-start.12 = (bf16[2,192,512]{2,1,0:T(8,128)(2,1)S(1)}, bf16[2,192,512]{2,1,0:T(8,128)(2,1)}, u32[]{:S(2)}) copy-start(bf16[2,192,512]{2,1,0:T(8,128)(2,1)} %get-tuple-element.47.v_t_ref) | copy-start | bytes 1179652
  151.7 7.5 %copy-start = (f32[2,32,512]{2,1,0:T(8,128)S(1)}, f32[2,32,512]{2,1,0:T(8,128)}, u32[]{:S(2)}) copy-start(f32[2,32,512]{2,1,0:T(8,128)} %get-tuple-element.92.sin_ref) | copy-start | bytes 393220
  151.7 7.5 %copy-start.1 = (f32[2,32,512]{2,1,0:T(8,128)S(1)}, f32[2,32,512]{2,1,0:T(8,128)}, u32[]{:S(2)}) copy-start(f32[2,32,512]{2,1,0:T(8,128)} %get-tuple-element.93.cos_ref) | copy-start | bytes 393220
  151.8 7.5 %copy-start.5 = (bf16[2,576,512]{2,1,0:T(8,128)(2,1)S(1)}, bf16[2,576,512]{2,1,0:T(8,128)(2,1)}, u32[]{:S(2)}) copy-start(bf16[2,576,512]{2,1,0:T(8,128)(2,1)} %get-tuple-element.45.q_t_ref) | copy-start | bytes 3538948
  151.8 7.6 %copy-start.6 = (bf16[2,576,512]{2,1,0:T(8,128)(2,1)S(1)}, bf16[2,576,512]{2,1,0:T(8,128)(2,1)}, u32[]{:S(2)}) copy-start(bf16[2,576,512]{2,1,0:T(8,128)(2,1)} %get-tuple-element.38.o_t_ref) | copy-start | bytes 3538948
  151.8 7.6 %copy-start.11 = (bf16[2,192,512]{2,1,0:T(8,128)(2,1)S(1)}, bf16[2,192,512]{2,1,0:T(8,128)(2,1)}, u32[]{:S(2)}) copy-start(bf16[2,192,512]{2,1,0:T(8,128)(2,1)} %get-tuple-element.46.k_t_ref) | copy-start | bytes 1179652
  154.0 23.2 %collective-permute-start.2 = (bf16[2,4,96,128]{3,2,1,0:T(8,128)(2,1)S(1)}, bf16[2,4,96,128]{3,2,1,0:T(8,128)(2,1)S(1)}, u32[]{:S(2)}, u32[]{:S(2)}) collective-permute-start(bf16[2,4,96,128]{3,2,1,0:T(8,128)(2,1)S(1)} %bitcast.110), channel_id=1, source_target_pairs={{0,2},{1,3},{2,4},{3,5},{4,6},{5,7},{6,0},{7,1},{8,10},{9,11},{10,... | collective-permute-start | bytes 589832 | tf_op jit(solution)/shard_map/ppermute | solution.py:576
  154.1 23.4 %collective-permute-start.3 = (bf16[2,4,96,128]{3,2,1,0:T(8,128)(2,1)S(1)}, bf16[2,4,96,128]{3,2,1,0:T(8,128)(2,1)S(1)}, u32[]{:S(2)}, u32[]{:S(2)}) collective-permute-start(bf16[2,4,96,128]{3,2,1,0:T(8,128)(2,1)S(1)} %bitcast.109), channel_id=1, source_target_pairs={{0,6},{1,7},{2,0},{3,1},{4,2},{5,3},{6,4},{7,5},{8,14},{9,15},{10,... | collective-permute-start | bytes 589832 | tf_op jit(solution)/shard_map/ppermute | solution.py:576
  159.3 1.3 copy-start.7
  160.6 8.9 %copy-start.16 = (bf16[64,96,128]{2,1,0:T(8,128)(2,1)S(1)}, bf16[64,96,128]{2,1,0:T(8,128)(2,1)}, u32[]{:S(2)}) copy-start(bf16[64,96,128]{2,1,0:T(8,128)(2,1)} %get-tuple-element.51) | copy-start | bytes 4718596
  169.5 2.2 copy-start.15
  173.9 12.3 %copy-start.13 = (f32[1152,1]{1,0:T(8,128)S(1)}, f32[1152,1]{1,0:T(8,128)}, u32[]{:S(2)}) copy-start(f32[1152,1]{1,0:T(8,128)} %get-tuple-element.39.gain_ref) | copy-start | bytes 13828
  173.9 8.5 %collective-permute-start.4 = (bf16[2,4,112,128]{3,2,1,0:T(8,128)(2,1)S(1)}, bf16[2,4,112,128]{3,2,1,0:T(8,128)(2,1)S(1)}, u32[]{:S(2)}, u32[]{:S(2)}) collective-permute-start(bf16[2,4,112,128]{3,2,1,0:T(8,128)(2,1)S(1)} %bitcast.105), channel_id=1, source_target_pairs={{0,8},{1,9},{2,10},{3,11},{4,12},{5,13},{6,14},{7,15},{8,16},{9,17... | collective-permute-start | bytes 688136 | tf_op jit(solution)/shard_map/ppermute | solution.py:576
  174.2 8.4 %collective-permute-start.5 = (bf16[2,4,112,128]{3,2,1,0:T(8,128)(2,1)S(1)}, bf16[2,4,112,128]{3,2,1,0:T(8,128)(2,1)S(1)}, u32[]{:S(2)}, u32[]{:S(2)}) collective-permute-start(bf16[2,4,112,128]{3,2,1,0:T(8,128)(2,1)S(1)} %bitcast.104), channel_id=1, source_target_pairs={{0,24},{1,25},{2,26},{3,27},{4,28},{5,29},{6,30},{7,31},{8,0},{9,1... | collective-permute-start | bytes 688136 | tf_op jit(solution)/shard_map/ppermute | solution.py:576
  177.3 8.9 %copy-start.10 = (bf16[2,576,512]{2,1,0:T(8,128)(2,1)S(1)}, bf16[2,576,512]{2,1,0:T(8,128)(2,1)}, u32[]{:S(2)}) copy-start(bf16[2,576,512]{2,1,0:T(8,128)(2,1)} %get-tuple-element.43.h_t_ref) | copy-start | bytes 3538948
  177.3 8.9 %copy-start.9 = (bf16[576,960]{1,0:T(8,128)(2,1)S(1)}, bf16[576,960]{1,0:T(8,128)(2,1)}, u32[]{:S(2)}) copy-start(bf16[576,960]{1,0:T(8,128)(2,1)} %get-tuple-element.41.w_ref) | copy-start | bytes 3317764
  177.4 21.4 %collective-permute-start.6 = (bf16[4,4,96,128]{3,2,1,0:T(8,128)(2,1)S(1)}, bf16[4,4,96,128]{3,2,1,0:T(8,128)(2,1)S(1)}, u32[]{:S(2)}, u32[]{:S(2)}) collective-permute-start(bf16[4,4,96,128]{3,2,1,0:T(8,128)(2,1)S(1)} %pad_maximum_fusion.4.rest_0_), channel_id=1, source_target_pairs={{0,2},{1,3},{2,4},{3,5},{4,6},{5,7},{6,0},{7,1},{8,10},{9,11},{10,... | collective-permute-start | bytes 1179656 | tf_op jit(solution)/shard_map/ppermute | solution.py:576
  177.5 8.8 %copy-start.8 = (bf16[960,512]{1,0:T(8,128)(2,1)S(1)}, bf16[960,512]{1,0:T(8,128)(2,1)}, u32[]{:S(2)}) copy-start(bf16[960,512]{1,0:T(8,128)(2,1)} %get-tuple-element.50.dqkv0_ref) | copy-start | bytes 2949124
  177.6 8.7 %copy-start.14 = (f32[576,1]{1,0:T(8,128)S(1)}, f32[576,1]{1,0:T(8,128)}, u32[]{:S(2)}) copy-start(f32[576,1]{1,0:T(8,128)} %get-tuple-element.42.dgain_two_ref) | copy-start | bytes 6916
  177.6 21.1 %collective-permute-start.7 = (bf16[4,4,96,128]{3,2,1,0:T(8,128)(2,1)S(1)}, bf16[4,4,96,128]{3,2,1,0:T(8,128)(2,1)S(1)}, u32[]{:S(2)}, u32[]{:S(2)}) collective-permute-start(bf16[4,4,96,128]{3,2,1,0:T(8,128)(2,1)S(1)} %pad_maximum_fusion.5.rest_1_), channel_id=1, source_target_pairs={{0,6},{1,7},{2,0},{3,1},{4,2},{5,3},{6,4},{7,5},{8,14},{9,15},{10,... | collective-permute-start | bytes 1179656 | tf_op jit(solution)/shard_map/ppermute | solution.py:576
  182.4 3.9 %copy-start.4 = (f32[2,576,512]{2,1,0:T(8,128)S(1)}, f32[2,576,512]{2,1,0:T(8,128)}, u32[]{:S(2)}) copy-start(f32[2,576,512]{2,1,0:T(8,128)} %get-tuple-element.44.dx1_ref) | copy-start | bytes 7077892
  182.4 3.8 %copy-start.2 = (s32[4]{0:T(128)S(1)}, s32[4]{0:T(128)}, u32[]{:S(2)}) copy-start(s32[4]{0:T(128)} %pad_add_fusion.where_ref) | copy-start | bytes 52
  182.5 3.8 %copy-start.3 = (bf16[2,512,576]{1,2,0:T(8,128)(2,1)S(1)}, bf16[2,512,576]{1,2,0:T(8,128)(2,1)}, u32[]{:S(2)}) copy-start(bf16[2,512,576]{1,2,0:T(8,128)(2,1)} %param.11) | copy-start | bytes 3538948
  182.5 16.4 %collective-permute-start.15 = (bf16[4,4,112,128]{3,2,1,0:T(8,128)(2,1)S(1)}, bf16[4,4,112,128]{3,2,1,0:T(8,128)(2,1)S(1)}, u32[]{:S(2)}, u32[]{:S(2)}) collective-permute-start(bf16[4,4,112,128]{3,2,1,0:T(8,128)(2,1)S(1)} %pad_maximum_fusion.2.rest_2_), channel_id=1, source_target_pairs={{0,8},{1,9},{2,10},{3,11},{4,12},{5,13},{6,14},{7,15},{8,16},{9,17... | collective-permute-start | bytes 1376264 | tf_op jit(solution)/shard_map/ppermute | solution.py:576
  182.7 16.2 %collective-permute-start.16 = (bf16[4,4,112,128]{3,2,1,0:T(8,128)(2,1)S(1)}, bf16[4,4,112,128]{3,2,1,0:T(8,128)(2,1)S(1)}, u32[]{:S(2)}, u32[]{:S(2)}) collective-permute-start(bf16[4,4,112,128]{3,2,1,0:T(8,128)(2,1)S(1)} %pad_maximum_fusion.3.rest_3_), channel_id=1, source_target_pairs={{0,24},{1,25},{2,26},{3,27},{4,28},{5,29},{6,30},{7,31},{8,0},{9,1... | collective-permute-start | bytes 1376264 | tf_op jit(solution)/shard_map/ppermute | solution.py:576
  195.2 3.9 %collective-permute-start.8 = (bf16[64,48,128]{2,1,0:T(8,128)(2,1)S(1)}, bf16[64,48,128]{2,1,0:T(8,128)(2,1)S(1)}, u32[]{:S(2)}, u32[]{:S(2)}) collective-permute-start(bf16[64,48,128]{2,1,0:T(8,128)(2,1)S(1)} %get-tuple-element.61), channel_id=1, source_target_pairs={{0,1},{1,0},{2,3},{3,2},{4,5},{5,4},{6,7},{7,6},{8,9},{9,8},{10,11... | collective-permute-start | bytes 2359304 | tf_op jit(solution)/shard_map/ppermute | solution.py:576
  199.4 7.8 %collective-permute-start.11 = (bf16[4,4,48,128]{3,2,1,0:T(8,128)(2,1)S(1)}, bf16[4,4,48,128]{3,2,1,0:T(8,128)(2,1)S(1)}, u32[]{:S(2)}, u32[]{:S(2)}) collective-permute-start(bf16[4,4,48,128]{3,2,1,0:T(8,128)(2,1)S(1)} %bitcast.108), channel_id=1, source_target_pairs={{0,6},{1,7},{2,0},{3,1},{4,2},{5,3},{6,4},{7,5},{8,14},{9,15},{10,... | collective-permute-start | bytes 589832 | tf_op jit(solution)/shard_map/ppermute | solution.py:576
  199.7 9.3 %collective-permute-start.9 = (bf16[4,4,48,128]{3,2,1,0:T(8,128)(2,1)S(1)}, bf16[4,4,48,128]{3,2,1,0:T(8,128)(2,1)S(1)}, u32[]{:S(2)}, u32[]{:S(2)}) collective-permute-start(bf16[4,4,48,128]{3,2,1,0:T(8,128)(2,1)S(1)} %bitcast.107), channel_id=1, source_target_pairs={{0,4},{1,5},{2,6},{3,7},{4,0},{5,1},{6,2},{7,3},{8,12},{9,13},{10,... | collective-permute-start | bytes 589832 | tf_op jit(solution)/shard_map/ppermute | solution.py:576
  200.6 12.6 %collective-permute-start.10 = (bf16[4,4,48,128]{3,2,1,0:T(8,128)(2,1)S(1)}, bf16[4,4,48,128]{3,2,1,0:T(8,128)(2,1)S(1)}, u32[]{:S(2)}, u32[]{:S(2)}) collective-permute-start(bf16[4,4,48,128]{3,2,1,0:T(8,128)(2,1)S(1)} %bitcast.106), channel_id=1, source_target_pairs={{0,2},{1,3},{2,4},{3,5},{4,6},{5,7},{6,0},{7,1},{8,10},{9,11},{10,... | collective-permute-start | bytes 589832 | tf_op jit(solution)/shard_map/ppermute | solution.py:576
  201.5 14.2 %collective-permute-start.17 = (bf16[4,112,128]{2,1,0:T(8,128)(2,1)S(1)}, bf16[4,112,128]{2,1,0:T(8,128)(2,1)S(1)}, u32[]{:S(2)}, u32[]{:S(2)}) collective-permute-start(bf16[4,112,128]{2,1,0:T(8,128)(2,1)S(1)} %get-tuple-element.76), channel_id=1, source_target_pairs={{0,4},{1,5},{2,6},{3,7},{4,0},{5,1},{6,2},{7,3},{8,12},{9,13},{10,... | collective-permute-start | bytes 344072 | tf_op jit(solution)/shard_map/ppermute | solution.py:576
  205.7 10.2 %collective-permute-start.19 = (bf16[4,112,128]{2,1,0:T(8,128)(2,1)S(1)}, bf16[4,112,128]{2,1,0:T(8,128)(2,1)S(1)}, u32[]{:S(2)}, u32[]{:S(2)}) collective-permute-start(bf16[4,112,128]{2,1,0:T(8,128)(2,1)S(1)} %get-tuple-element.77), channel_id=1, source_target_pairs={{0,6},{1,7},{2,0},{3,1},{4,2},{5,3},{6,4},{7,5},{8,14},{9,15},{10,... | collective-permute-start | bytes 344072 | tf_op jit(solution)/shard_map/ppermute | solution.py:576
  207.1 10.3 %collective-permute-start.18 = (bf16[4,112,128]{2,1,0:T(8,128)(2,1)S(1)}, bf16[4,112,128]{2,1,0:T(8,128)(2,1)S(1)}, u32[]{:S(2)}, u32[]{:S(2)}) collective-permute-start(bf16[4,112,128]{2,1,0:T(8,128)(2,1)S(1)} %get-tuple-element.78), channel_id=1, source_target_pairs={{0,2},{1,3},{2,4},{3,5},{4,6},{5,7},{6,0},{7,1},{8,10},{9,11},{10,... | collective-permute-start | bytes 344072 | tf_op jit(solution)/shard_map/ppermute | solution.py:576
  213.5 8.3 %collective-permute-start.12 = (bf16[4,144,128]{2,1,0:T(8,128)(2,1)S(1)}, bf16[4,144,128]{2,1,0:T(8,128)(2,1)S(1)}, u32[]{:S(2)}, u32[]{:S(2)}) collective-permute-start(bf16[4,144,128]{2,1,0:T(8,128)(2,1)S(1)} %get-tuple-element.73), channel_id=1, source_target_pairs={{0,16},{1,17},{2,18},{3,19},{4,20},{5,21},{6,22},{7,23},{8,24},{9,... | collective-permute-start | bytes 442376 | tf_op jit(solution)/shard_map/ppermute | solution.py:576
  213.6 8.2 %collective-permute-start.14 = (bf16[4,144,128]{2,1,0:T(8,128)(2,1)S(1)}, bf16[4,144,128]{2,1,0:T(8,128)(2,1)S(1)}, u32[]{:S(2)}, u32[]{:S(2)}) collective-permute-start(bf16[4,144,128]{2,1,0:T(8,128)(2,1)S(1)} %get-tuple-element.74), channel_id=1, source_target_pairs={{0,24},{1,25},{2,26},{3,27},{4,28},{5,29},{6,30},{7,31},{8,0},{9,1... | collective-permute-start | bytes 442376 | tf_op jit(solution)/shard_map/ppermute | solution.py:576
  215.7 8.1 %collective-permute-start.13 = (bf16[4,144,128]{2,1,0:T(8,128)(2,1)S(1)}, bf16[4,144,128]{2,1,0:T(8,128)(2,1)S(1)}, u32[]{:S(2)}, u32[]{:S(2)}) collective-permute-start(bf16[4,144,128]{2,1,0:T(8,128)(2,1)S(1)} %get-tuple-element.75), channel_id=1, source_target_pairs={{0,8},{1,9},{2,10},{3,11},{4,12},{5,13},{6,14},{7,15},{8,16},{9,17... | collective-permute-start | bytes 442376 | tf_op jit(solution)/shard_map/ppermute | solution.py:576
  224.0 6.5 %collective-permute-start.20 = (bf16[256,128]{1,0:T(8,128)(2,1)S(1)}, bf16[256,128]{1,0:T(8,128)(2,1)S(1)}, u32[]{:S(2)}, u32[]{:S(2)}) collective-permute-start(bf16[256,128]{1,0:T(8,128)(2,1)S(1)} %get-tuple-element.83), channel_id=1, source_target_pairs={{0,64},{1,65},{2,66},{3,67},{4,68},{5,69},{6,70},{7,71},{8,72},{9,... | collective-permute-start | bytes 196616 | tf_op jit(solution)/shard_map/ppermute | solution.py:576
  226.2 4.3 %collective-permute-start.22 = (bf16[256,128]{1,0:T(8,128)(2,1)S(1)}, bf16[256,128]{1,0:T(8,128)(2,1)S(1)}, u32[]{:S(2)}, u32[]{:S(2)}) collective-permute-start(bf16[256,128]{1,0:T(8,128)(2,1)S(1)} %get-tuple-element.84), channel_id=1, source_target_pairs={{0,96},{1,97},{2,98},{3,99},{4,100},{5,101},{6,102},{7,103},{8,104... | collective-permute-start | bytes 196616 | tf_op jit(solution)/shard_map/ppermute | solution.py:576
  227.4 5.5 %collective-permute-start.21 = (bf16[256,128]{1,0:T(8,128)(2,1)S(1)}, bf16[256,128]{1,0:T(8,128)(2,1)S(1)}, u32[]{:S(2)}, u32[]{:S(2)}) collective-permute-start(bf16[256,128]{1,0:T(8,128)(2,1)S(1)} %get-tuple-element.85), channel_id=1, source_target_pairs={{0,32},{1,33},{2,34},{3,35},{4,36},{5,37},{6,38},{7,39},{8,40},{9,... | collective-permute-start | bytes 196616 | tf_op jit(solution)/shard_map/ppermute | solution.py:576
Sparse Core Ops, SparseCore 0:
  16.0 82.9 all-gather.2

commit v3 on v2

--- a/solution.py
+++ b/solution.py
@@ -1,3 +1,5 @@
+import functools
+
 import jax
 import jax.numpy as jnp
 from jax import lax
@@ -84,38 +86,25 @@
             ref[pl.ds(3 * half + j, D, stride=6), :width] = val_ref[:, at : at + width]
 
 
-def pack_kernel(wqo, wkv, gn, wd, wgu, f_ref, q_ref, f_stage_ref, q_stage_ref):
-    f_stage_ref[...] = jnp.zeros_like(f_stage_ref)
-    q_stage_ref[...] = jnp.zeros_like(q_stage_ref)
-    square = wqo[...].astype(F32)
-    thin = wkv[...].astype(F32)
-    for ref, at, val in (
-        (q_stage_ref, Q_QUERY, square[:R_OUT]),
-        (q_stage_ref, Q_KEY, thin[:R_KEY]),
-        (q_stage_ref, Q_VALUE, thin[R_KEY:]),
-        (q_stage_ref, Q_GAIN, gn[...].astype(F32)),
-        (f_stage_ref, F_GATE, wgu[...].astype(F32)),
-        (f_stage_ref, F_DOWN, wd[...].astype(F32)),
-        (f_stage_ref, F_OUT, square[R_OUT:]),
-    ):
-        ref[at : at + val.shape[0], : val.shape[1]] = val
-    f_ref[...] = f_stage_ref[...].astype(BF16)
-    q_ref[...] = q_stage_ref[...].astype(BF16)
-
-
-def pack(pieces):
+def pack_kernel(starts, count, *refs):
+    out_ref, stage_ref = refs[-2:]
+    stage_ref[...] = jnp.zeros_like(stage_ref)
+    for at, ref in zip(starts, refs[:count]):
+        val = ref[...].astype(F32)
+        stage_ref[at : at + val.shape[0], : val.shape[1]] = val
+    out_ref[...] = stage_ref[...].astype(BF16)
+
+
+def pack(pieces, starts, rows, after):
     vmem = pl.BlockSpec(memory_space=pltpu.VMEM)
     return pl.pallas_call(
-        pack_kernel,
-        in_specs=[vmem] * 5,
-        out_specs=[vmem] * 2,
-        out_shape=[
-            jax.ShapeDtypeStruct((ROWS_F, 128), BF16),
-            jax.ShapeDtypeStruct((ROWS_Q, 128), BF16),
-        ],
-        scratch_shapes=[pltpu.VMEM((ROWS_F, 128), F32), pltpu.VMEM((ROWS_Q, 128), F32)],
+        functools.partial(pack_kernel, starts, len(pieces)),
+        in_specs=[vmem] * len(pieces) + [pl.BlockSpec(memory_space=pl.ANY)] * len(after),
+        out_specs=vmem,
+        out_shape=jax.ShapeDtypeStruct((rows, 128), BF16),
+        scratch_shapes=[pltpu.VMEM((rows, 128), F32)],
         name="pack",
-    )(*pieces)
+    )(*pieces, *after)
 
 
 def lane_rows(v, rows, width):
@@ -612,14 +601,27 @@
     x_t = jnp.swapaxes(tokens, 1, 2)
     cot_t = jnp.swapaxes(cotangent, 1, 2)
 
-    pack_f, pack_q = pack(
+    pack_f = pack(
         [
-            lane_rows(jnp.concatenate([w_query, w_out]), 18, 288),
-            jnp.concatenate([w_key, w_value]).reshape(18, 96),
+            w_gate.reshape(R_GATE, 128),
+            w_up.reshape(R_GATE, 128),
+            lane_rows(w_down, 12, D),
+            lane_rows(w_out, 9, 288),
+        ],
+        (F_GATE, F_UP, F_DOWN, F_OUT),
+        ROWS_F,
+        [],
+    )
+    pack_q = pack(
+        [
+            lane_rows(w_query, 9, 288),
+            w_key.reshape(9, 96),
+            w_value.reshape(9, 96),
             norm_gains.reshape(1, 9),
-            lane_rows(w_down, 12, D),
-            jnp.concatenate([w_gate, w_up]).reshape(2 * R_GATE, 128),
-        ]
+        ],
+        (Q_QUERY, Q_KEY, Q_VALUE, Q_GAIN),
+        ROWS_Q,
+        [pack_f],
     )
     all_f = lax.all_gather(pack_f, "dp", axis=0, tiled=False)
     all_q = lax.all_to_all(

time: 245 us -> 242 us (0.988)
  waiting for transfers between devices: 63.7 us -> 59 us
    all_gather x1, waiting for transfers between devices: 21.6 us -> 17.2 us  [on_device(): all_f = lax.all_gather(pack_f, 'dp', axis=0, tiled=False)]
    concatenate x4 -> x0, local copies, waits for them, and re-layouts: 3.1 us -> none  [the longest x2 1.56 us: on_device(): jnp.concatenate([w_query, w_out])]
    reshape x0 -> x2, local copies, waits for them, and re-layouts: none -> 2.72 us  [the longest x1 1.36 us: on_device(): w_key.reshape(9, 96)]
  transfers between devices with their start and end apart: 25 -> 25, of which waited for: 13 -> 13; matrix products, arithmetic and copies ran while one was open for 9% -> 11% of each run, Pallas kernels for 20% -> 21%
where the time goes in v3:
time: 242 us; the launch traced here: 241 us
  Pallas kernels  93.5 us (39%)
  waiting for transfers between devices  59 us (24%)
  starting transfers between devices  38.8 us (16%)
  local copies, waits for them, and re-layouts  19 us (8%)
  other arithmetic  15.9 us (7%)
  between operations  14.7 us (6%)
    pallas_call x1, Pallas kernels, ffn(): pl.pallas_call(ffn_kernel, in_specs=[pl.BlockSpec(memory_space=pltpu.SMEM...  41.2 us
    ppermute x23, starting transfers between devices, hop(): return lax.ppermute(v, 'dp', pairs(axis, step))  27.2 us
    pallas_call x1, Pallas kernels, attn_fwd(): pl.pallas_call(attn_fwd_kernel, grid=(seqs,), in_specs=[whole_spec((2 * C...  22.9 us
    ppermute x23, waiting for transfers between devices, hop(): return lax.ppermute(v, 'dp', pairs(axis, step))  21.4 us
    all_to_all x1, waiting for transfers between devices, on_device(): lax.all_to_all(jnp.broadcast_to(pack_q[None], (2 * CHIPS, ROWS_Q, 128)),...  20.4 us
    pallas_call x2, Pallas kernels, attn_bwd(): pl.pallas_call(attn_bwd_kernel, grid=(1,), in_specs=[seq_spec((32, SEQ),...  18.3 us
    all_gather x1, waiting for transfers between devices, on_device(): all_f = lax.all_gather(pack_f, 'dp', axis=0, tiled=False)  17.2 us
    all_to_all x1, starting transfers between devices, on_device(): lax.all_to_all(jnp.broadcast_to(pack_q[None], (2 * CHIPS, ROWS_Q, 128)),...  11.6 us
  transfers between devices with their start and end apart: 25, of which 13 were waited for; matrix products, arithmetic and copies ran while one was open for 11% of the time, Pallas kernels for 21%

profile of v3, /device:TPU:0, one launch (start us, length us, event | category | flops | bytes accessed | tf_op | source)
XLA Modules:
  0.0 240.9 jit_solution(10796190216608431062)
XLA Ops:
  7.2 0.8 reshape.265
  8.6 0.8 reshape.263
  10.1 1.4 pack.2.refs_4_
  11.5 1.4 reshape.269.refs_1_
  12.9 1.4 reshape.270.refs_2_
  14.2 0.8 reshape.267
  15.6 1.3 pack.3
  17.0 2.1 broadcast_in_dim.2
  19.0 11.6 %all-to-all-start = ((bf16[128,48,128]{2,1,0:T(8,128)(2,1)}), bf16[128,48,128]{2,1,0:T(8,128)(2,1)}, u32[]{:S(2)}, u32[]{:S(2)}) async-start(bf16[128,48,128]{2,1,0:T(8,128)(2,1)} %broadcast_in_dim.2), calls=%async_computation | async-start | bytes 3145728 | tf_op jit(solution)/shard_map/all_to_all | solution.py:627
  32.0 1.1 reduce_window_sum.34.docc_ref
  33.7 1.3 multiply_sine_fusion
  35.0 20.4 %all-to-all-done.pack_ref = bf16[128,48,128]{2,1,0:T(8,128)(2,1)} async-done(((bf16[128,48,128]{2,1,0:T(8,128)(2,1)}), bf16[128,48,128]{2,1,0:T(8,128)(2,1)}, u32[]{:S(2)}, u32[]{:S(2)}) %all-to-all-start) | async-done | bytes 1572896 | tf_op jit(solution)/shard_map/all_to_all | solution.py:627
  55.4 22.9 %attn_fwd.1 = (bf16[576,960]{1,0:T(8,128)(2,1)}, f32[1152,1]{1,0:T(8,128)}, bf16[2,576,512]{2,1,0:T(8,128)(2,1)}, bf16[2,576,512]{2,1,0:T(8,128)(2,1)}, bf16[2,1...) custom-call(bf16[128,48,128]{2,1,0:T(8,128)(2,1)} %all-to-all-done.p, ...), custom_call_target="tpu_custom_call" | custom-call | flops 8000000000 | bytes 20000000 | tf_op jit(solution)/shard_map/attn_fwd/pallas_call | solution.py:210
  78.3 17.2 %all-gather.3.cloned.1.call-done = bf16[26624,128]{1,0:T(8,128)(2,1)} async-done(((bf16[208,128]{1,0:T(8,128)(2,1)}), bf16[26624,128]{1,0:T(8,128)(2,1)}) %all-gather.3.cloned.1.call-update) | async-done | bytes 6815760 | tf_op jit(solution)/shard_map/all_gather | solution.py:626
  95.5 41.2 %ffn.1 = (bf16[2,576,512]{2,1,0:T(8,128)(2,1)}, f32[2,576,512]{2,1,0:T(8,128)}, bf16[2,576,512]{2,1,0:T(8,128)(2,1)}, f32[576,1]{1,0:T(8,128)}, bf16[64,96,128]{...) custom-call(s32[4]{0:T(128)} %pad_add_fusion.where_ref, ...), custom_call_target="tpu_custom_call" | custom-call | flops 24999999488 | bytes 30000000 | tf_op jit(solution)/shard_map/ffn/pallas_call | solution.py:361
  137.2 9.9 %attn_bwd.2 = (bf16[960,512]{1,0:T(8,128)(2,1)}, f32[8,128]{1,0:T(8,128)}) custom-call(f32[2,32,512]{2,1,0:T(8,128)} %get-tuple-element.89.cos_ref, f32[2,32,512]{2,1,0:T(8,128)} %get-tuple-element.88.sin_ref, bf16[2,576,512]{2,1,0:T(8,128)(2,1)} %get-tuple-element.41.q_t_ref, bf16[2,192,512]{2,1,0:T(8,128)(2,1)} %get-tuple-element.42.k_t_ref, ...), custom_call_target="tpu_custom_call" | custom-call | flops 8000000000 | bytes 8000000 | tf_op jit(solution)/shard_map/attn_bwd/pallas_call | solution.py:445
  147.1 1.2 slice.295
  148.3 2.2 add_convert_fusion.1
  150.6 3.2 %collective-permute-start.3 = (bf16[2,4,96,128]{3,2,1,0:T(8,128)(2,1)S(1)}, bf16[2,4,96,128]{3,2,1,0:T(8,128)(2,1)S(1)}, u32[]{:S(2)}, u32[]{:S(2)}) collective-permute-start(bf16[2,4,96,128]{3,2,1,0:T(8,128)(2,1)S(1)} %bitcast.109), channel_id=1, source_target_pairs={{0,6},{1,7},{2,0},{3,1},{4,2},{5,3},{6,4},{7,5},{8,14},{9,15},{10,... | collective-permute-start | bytes 589832 | tf_op jit(solution)/shard_map/ppermute | solution.py:565
  153.9 2.0 add_convert_fusion
  155.9 1.3 copy-done.7
  157.2 8.3 %attn_bwd.3 = (bf16[960,512]{1,0:T(8,128)(2,1)S(1)}, f32[8,128]{1,0:T(8,128)S(1)}) custom-call(f32[2,32,512]{2,1,0:T(8,128)S(1)} %copy-done.1, f32[2,32,512]{2,1,0:T(8,128)S(1)} %copy-done, bf16[2,576,512]{2,1,0:T(8,128)(2,1)S(1)} %copy-done.5, bf16[2,192,512]{2,1,0:T(8,128)(2,1)S(1)} %copy-done.11, bf16[2,192,512]{2,1,0:T(8,128)(2,1)S(1)} %copy-done.12, ...), custom_call_target="tpu_custom_call" | custom-call | flops 8000000000 | bytes 8000000 | tf_op jit(solution)/shard_map/attn_bwd/pallas_call | solution.py:445
  166.0 2.1 add_add_fusion.4
  168.2 2.0 add_add_fusion.1
  170.8 3.0 %collective-permute-start.5 = (bf16[2,4,112,128]{3,2,1,0:T(8,128)(2,1)S(1)}, bf16[2,4,112,128]{3,2,1,0:T(8,128)(2,1)S(1)}, u32[]{:S(2)}, u32[]{:S(2)}) collective-permute-start(bf16[2,4,112,128]{3,2,1,0:T(8,128)(2,1)S(1)} %bitcast.104), channel_id=1, source_target_pairs={{0,24},{1,25},{2,26},{3,27},{4,28},{5,29},{6,30},{7,31},{8,0},{9,1... | collective-permute-start | bytes 688136 | tf_op jit(solution)/shard_map/ppermute | solution.py:565
  174.2 3.3 %collective-permute-start.7 = (bf16[4,4,96,128]{3,2,1,0:T(8,128)(2,1)S(1)}, bf16[4,4,96,128]{3,2,1,0:T(8,128)(2,1)S(1)}, u32[]{:S(2)}, u32[]{:S(2)}) collective-permute-start(bf16[4,4,96,128]{3,2,1,0:T(8,128)(2,1)S(1)} %pad_maximum_fusion.5.rest_1_), channel_id=1, source_target_pairs={{0,6},{1,7},{2,0},{3,1},{4,2},{5,3},{6,4},{7,5},{8,14},{9,15},{10,... | collective-permute-start | bytes 1179656 | tf_op jit(solution)/shard_map/ppermute | solution.py:565
  177.4 1.5 collective-permute-done.4
  179.3 3.5 %collective-permute-start.16 = (bf16[4,4,112,128]{3,2,1,0:T(8,128)(2,1)S(1)}, bf16[4,4,112,128]{3,2,1,0:T(8,128)(2,1)S(1)}, u32[]{:S(2)}, u32[]{:S(2)}) collective-permute-start(bf16[4,4,112,128]{3,2,1,0:T(8,128)(2,1)S(1)} %pad_maximum_fusion.3.rest_3_), channel_id=1, source_target_pairs={{0,24},{1,25},{2,26},{3,27},{4,28},{5,29},{6,30},{7,31},{8,0},{9,1... | collective-permute-start | bytes 1376264 | tf_op jit(solution)/shard_map/ppermute | solution.py:565
  182.8 8.4 %qkv_bwd.1 = (f32[2,576,512]{2,1,0:T(8,128)}, bf16[64,48,128]{2,1,0:T(8,128)(2,1)S(1)}, bf16[64,48,128]{2,1,0:T(8,128)(2,1)S(1)}, f32[8,128]{1,0:T(8,128)S(1)}) custom-call(s32[4]{0:T(128)S(1)} %copy-done.2, bf16[576,960]{1,0:T(8,128)(2,1)S(1)} %copy-done.9, f32[1152,1]{1,0:T(8,128)S(1)} %copy-done.13, f32[576,1]{1,0:T(8,128)S(1)} %copy-done.14, ...), custom_call_target="tpu_custom_call" | custom-call | flops 8000000000 | bytes 12000000 | tf_op jit(solution)/shard_map/qkv_bwd/pallas_call | solution.py:524
  191.8 1.8 add_add_fusion
  193.6 1.7 add_add_fusion.3
  196.3 0.9 collective-permute-start.9
  197.2 0.8 collective-permute-start.10
  198.1 4.2 %collective-permute-start.17 = (bf16[4,112,128]{2,1,0:T(8,128)(2,1)S(1)}, bf16[4,112,128]{2,1,0:T(8,128)(2,1)S(1)}, u32[]{:S(2)}, u32[]{:S(2)}) collective-permute-start(bf16[4,112,128]{2,1,0:T(8,128)(2,1)S(1)} %get-tuple-element.72), channel_id=1, source_target_pairs={{0,4},{1,5},{2,6},{3,7},{4,0},{5,1},{6,2},{7,3},{8,12},{9,13},{10,... | collective-permute-start | bytes 344072 | tf_op jit(solution)/shard_map/ppermute | solution.py:565
  202.6 1.1 collective-permute-done.11
  203.7 0.7 collective-permute-start.18
  204.4 1.1 collective-permute-done.9
  205.6 4.2 %collective-permute-done.10 = bf16[4,4,48,128]{3,2,1,0:T(8,128)(2,1)S(1)} collective-permute-done((bf16[4,4,48,128]{3,2,1,0:T(8,128)(2,1)S(1)}, bf16[4,4,48,128]{3,2,1,0:T(8,128)(2,1)S(1)}, u32[]{:S(2)}, u32[]{:S(2)}) %collective-permute-start.10) | collective-permute-done | bytes 196640 | tf_op jit(solution)/shard_map/ppermute | solution.py:565
  210.1 1.5 collective-permute-start.14
  212.5 1.6 collective-permute-done.18
  214.1 4.2 %collective-permute-done.12 = bf16[4,144,128]{2,1,0:T(8,128)(2,1)S(1)} collective-permute-done((bf16[4,144,128]{2,1,0:T(8,128)(2,1)S(1)}, bf16[4,144,128]{2,1,0:T(8,128)(2,1)S(1)}, u32[]{:S(2)}, u32[]{:S(2)}) %collective-permute-start.12) | collective-permute-done | bytes 147488 | tf_op jit(solution)/shard_map/ppermute | solution.py:565
  218.3 2.0 collective-permute-done.13
  220.5 2.2 collective-permute-start.20
  222.8 1.2 collective-permute-start.22
  223.9 0.8 collective-permute-start.21
  224.8 2.2 collective-permute-done.20
  227.0 2.4 collective-permute-done.21
  232.0 0.7 reshape.284
  (126 shorter events, 13.1 us)
Async XLA Ops:
  7.2 88.3 %all-gather.3.cloned.1.call-start = ((), (), s32[]{:S(2)}) async-start(), calls=%async_computation.1 | async-start | bytes 6868992 | tf_op jit(solution)/shard_map/all_gather | solution.py:626
  19.0 11.7 %copy-start.17 = (s32[2,512]{1,0:T(2,128)S(1)}, s32[2,512]{1,0:T(2,128)}, u32[]{:S(2)}) copy-start(s32[2,512]{1,0:T(2,128)} %param.12) | copy-start | bytes 12292
  19.0 36.4 %all-to-all-start = ((bf16[128,48,128]{2,1,0:T(8,128)(2,1)}), bf16[128,48,128]{2,1,0:T(8,128)(2,1)}, u32[]{:S(2)}, u32[]{:S(2)}) async-start(bf16[128,48,128]{2,1,0:T(8,128)(2,1)} %broadcast_in_dim.2), calls=%async_computation | async-start | bytes 3145728 | tf_op jit(solution)/shard_map/all_to_all | solution.py:627
  32.0 23.5 %copy-start.18 = (s32[2,4,128]{2,1,0:T(4,128)}, s32[2,4,128]{2,1,0:T(4,128)S(1)}, u32[]{:S(2)}) copy-start(s32[2,4,128]{2,1,0:T(4,128)S(1)} %broadcast_add_fusion) | copy-start | bytes 12292
  136.7 11.6 %collective-permute-start = (bf16[64,96,128]{2,1,0:T(8,128)(2,1)}, bf16[64,96,128]{2,1,0:T(8,128)(2,1)}, u32[]{:S(2)}, u32[]{:S(2)}) collective-permute-start(bf16[64,96,128]{2,1,0:T(8,128)(2,1)} %get-tuple-element.48), channel_id=1, source_target_pairs={{0,1},{1,0},{2,3},{3,2},{4,5},{5,4},{6,7},{7,6},{8,9},{9,8},{10,11... | collective-permute-start | bytes 4718600 | tf_op jit(solution)/shard_map/ppermute | solution.py:565
  136.9 16.9 %collective-permute-start.1 = (bf16[64,112,128]{2,1,0:T(8,128)(2,1)}, bf16[64,112,128]{2,1,0:T(8,128)(2,1)}, u32[]{:S(2)}, u32[]{:S(2)}) collective-permute-start(bf16[64,112,128]{2,1,0:T(8,128)(2,1)} %get-tuple-element.51), channel_id=1, source_target_pairs={{0,1},{1,0},{2,3},{3,2},{4,5},{5,4},{6,7},{7,6},{8,9},{9,8},{10,11... | collective-permute-start | bytes 5505032 | tf_op jit(solution)/shard_map/ppermute | solution.py:565
  137.2 18.7 %copy-start.12 = (bf16[2,192,512]{2,1,0:T(8,128)(2,1)S(1)}, bf16[2,192,512]{2,1,0:T(8,128)(2,1)}, u32[]{:S(2)}) copy-start(bf16[2,192,512]{2,1,0:T(8,128)(2,1)} %get-tuple-element.43.v_t_ref) | copy-start | bytes 1179652
  148.3 7.5 %copy-start = (f32[2,32,512]{2,1,0:T(8,128)S(1)}, f32[2,32,512]{2,1,0:T(8,128)}, u32[]{:S(2)}) copy-start(f32[2,32,512]{2,1,0:T(8,128)} %get-tuple-element.88.sin_ref) | copy-start | bytes 393220
  148.3 7.5 %copy-start.1 = (f32[2,32,512]{2,1,0:T(8,128)S(1)}, f32[2,32,512]{2,1,0:T(8,128)}, u32[]{:S(2)}) copy-start(f32[2,32,512]{2,1,0:T(8,128)} %get-tuple-element.89.cos_ref) | copy-start | bytes 393220
  148.3 7.5 %copy-start.5 = (bf16[2,576,512]{2,1,0:T(8,128)(2,1)S(1)}, bf16[2,576,512]{2,1,0:T(8,128)(2,1)}, u32[]{:S(2)}) copy-start(bf16[2,576,512]{2,1,0:T(8,128)(2,1)} %get-tuple-element.41.q_t_ref) | copy-start | bytes 3538948
  148.3 7.6 %copy-start.6 = (bf16[2,576,512]{2,1,0:T(8,128)(2,1)S(1)}, bf16[2,576,512]{2,1,0:T(8,128)(2,1)}, u32[]{:S(2)}) copy-start(bf16[2,576,512]{2,1,0:T(8,128)(2,1)} %get-tuple-element.34.o_t_ref) | copy-start | bytes 3538948
  148.3 7.6 %copy-start.11 = (bf16[2,192,512]{2,1,0:T(8,128)(2,1)S(1)}, bf16[2,192,512]{2,1,0:T(8,128)(2,1)}, u32[]{:S(2)}) copy-start(bf16[2,192,512]{2,1,0:T(8,128)(2,1)} %get-tuple-element.42.k_t_ref) | copy-start | bytes 1179652
  150.6 23.2 %collective-permute-start.2 = (bf16[2,4,96,128]{3,2,1,0:T(8,128)(2,1)S(1)}, bf16[2,4,96,128]{3,2,1,0:T(8,128)(2,1)S(1)}, u32[]{:S(2)}, u32[]{:S(2)}) collective-permute-start(bf16[2,4,96,128]{3,2,1,0:T(8,128)(2,1)S(1)} %bitcast.110), channel_id=1, source_target_pairs={{0,2},{1,3},{2,4},{3,5},{4,6},{5,7},{6,0},{7,1},{8,10},{9,11},{10,... | collective-permute-start | bytes 589832 | tf_op jit(solution)/shard_map/ppermute | solution.py:565
  150.6 23.4 %collective-permute-start.3 = (bf16[2,4,96,128]{3,2,1,0:T(8,128)(2,1)S(1)}, bf16[2,4,96,128]{3,2,1,0:T(8,128)(2,1)S(1)}, u32[]{:S(2)}, u32[]{:S(2)}) collective-permute-start(bf16[2,4,96,128]{3,2,1,0:T(8,128)(2,1)S(1)} %bitcast.109), channel_id=1, source_target_pairs={{0,6},{1,7},{2,0},{3,1},{4,2},{5,3},{6,4},{7,5},{8,14},{9,15},{10,... | collective-permute-start | bytes 589832 | tf_op jit(solution)/shard_map/ppermute | solution.py:565
  155.9 1.3 copy-start.7
  157.2 8.9 %copy-start.16 = (bf16[64,96,128]{2,1,0:T(8,128)(2,1)S(1)}, bf16[64,96,128]{2,1,0:T(8,128)(2,1)}, u32[]{:S(2)}) copy-start(bf16[64,96,128]{2,1,0:T(8,128)(2,1)} %get-tuple-element.47) | copy-start | bytes 4718596
  166.0 2.2 copy-start.15
  170.4 12.4 %copy-start.13 = (f32[1152,1]{1,0:T(8,128)S(1)}, f32[1152,1]{1,0:T(8,128)}, u32[]{:S(2)}) copy-start(f32[1152,1]{1,0:T(8,128)} %get-tuple-element.35.gain_ref) | copy-start | bytes 13828
  170.5 8.5 %collective-permute-start.4 = (bf16[2,4,112,128]{3,2,1,0:T(8,128)(2,1)S(1)}, bf16[2,4,112,128]{3,2,1,0:T(8,128)(2,1)S(1)}, u32[]{:S(2)}, u32[]{:S(2)}) collective-permute-start(bf16[2,4,112,128]{3,2,1,0:T(8,128)(2,1)S(1)} %bitcast.105), channel_id=1, source_target_pairs={{0,8},{1,9},{2,10},{3,11},{4,12},{5,13},{6,14},{7,15},{8,16},{9,17... | collective-permute-start | bytes 688136 | tf_op jit(solution)/shard_map/ppermute | solution.py:565
  170.8 8.4 %collective-permute-start.5 = (bf16[2,4,112,128]{3,2,1,0:T(8,128)(2,1)S(1)}, bf16[2,4,112,128]{3,2,1,0:T(8,128)(2,1)S(1)}, u32[]{:S(2)}, u32[]{:S(2)}) collective-permute-start(bf16[2,4,112,128]{3,2,1,0:T(8,128)(2,1)S(1)} %bitcast.104), channel_id=1, source_target_pairs={{0,24},{1,25},{2,26},{3,27},{4,28},{5,29},{6,30},{7,31},{8,0},{9,1... | collective-permute-start | bytes 688136 | tf_op jit(solution)/shard_map/ppermute | solution.py:565
  173.8 9.0 %copy-start.10 = (bf16[2,576,512]{2,1,0:T(8,128)(2,1)S(1)}, bf16[2,576,512]{2,1,0:T(8,128)(2,1)}, u32[]{:S(2)}) copy-start(bf16[2,576,512]{2,1,0:T(8,128)(2,1)} %get-tuple-element.39.h_t_ref) | copy-start | bytes 3538948
  173.9 8.9 %copy-start.9 = (bf16[576,960]{1,0:T(8,128)(2,1)S(1)}, bf16[576,960]{1,0:T(8,128)(2,1)}, u32[]{:S(2)}) copy-start(bf16[576,960]{1,0:T(8,128)(2,1)} %get-tuple-element.37.w_ref) | copy-start | bytes 3317764
  173.9 21.4 %collective-permute-start.6 = (bf16[4,4,96,128]{3,2,1,0:T(8,128)(2,1)S(1)}, bf16[4,4,96,128]{3,2,1,0:T(8,128)(2,1)S(1)}, u32[]{:S(2)}, u32[]{:S(2)}) collective-permute-start(bf16[4,4,96,128]{3,2,1,0:T(8,128)(2,1)S(1)} %pad_maximum_fusion.4.rest_0_), channel_id=1, source_target_pairs={{0,2},{1,3},{2,4},{3,5},{4,6},{5,7},{6,0},{7,1},{8,10},{9,11},{10,... | collective-permute-start | bytes 1179656 | tf_op jit(solution)/shard_map/ppermute | solution.py:565
  174.0 8.8 %copy-start.8 = (bf16[960,512]{1,0:T(8,128)(2,1)S(1)}, bf16[960,512]{1,0:T(8,128)(2,1)}, u32[]{:S(2)}) copy-start(bf16[960,512]{1,0:T(8,128)(2,1)} %get-tuple-element.46.dqkv0_ref) | copy-start | bytes 2949124
  174.1 8.7 %copy-start.14 = (f32[576,1]{1,0:T(8,128)S(1)}, f32[576,1]{1,0:T(8,128)}, u32[]{:S(2)}) copy-start(f32[576,1]{1,0:T(8,128)} %get-tuple-element.38.dgain_two_ref) | copy-start | bytes 6916
  174.2 21.2 %collective-permute-start.7 = (bf16[4,4,96,128]{3,2,1,0:T(8,128)(2,1)S(1)}, bf16[4,4,96,128]{3,2,1,0:T(8,128)(2,1)S(1)}, u32[]{:S(2)}, u32[]{:S(2)}) collective-permute-start(bf16[4,4,96,128]{3,2,1,0:T(8,128)(2,1)S(1)} %pad_maximum_fusion.5.rest_1_), channel_id=1, source_target_pairs={{0,6},{1,7},{2,0},{3,1},{4,2},{5,3},{6,4},{7,5},{8,14},{9,15},{10,... | collective-permute-start | bytes 1179656 | tf_op jit(solution)/shard_map/ppermute | solution.py:565
  179.0 3.9 %copy-start.4 = (f32[2,576,512]{2,1,0:T(8,128)S(1)}, f32[2,576,512]{2,1,0:T(8,128)}, u32[]{:S(2)}) copy-start(f32[2,576,512]{2,1,0:T(8,128)} %get-tuple-element.40.dx1_ref) | copy-start | bytes 7077892
  179.0 3.8 %copy-start.2 = (s32[4]{0:T(128)S(1)}, s32[4]{0:T(128)}, u32[]{:S(2)}) copy-start(s32[4]{0:T(128)} %pad_add_fusion.where_ref) | copy-start | bytes 52
  179.0 3.8 %copy-start.3 = (bf16[2,512,576]{1,2,0:T(8,128)(2,1)S(1)}, bf16[2,512,576]{1,2,0:T(8,128)(2,1)}, u32[]{:S(2)}) copy-start(bf16[2,512,576]{1,2,0:T(8,128)(2,1)} %param.11) | copy-start | bytes 3538948
  179.1 16.4 %collective-permute-start.15 = (bf16[4,4,112,128]{3,2,1,0:T(8,128)(2,1)S(1)}, bf16[4,4,112,128]{3,2,1,0:T(8,128)(2,1)S(1)}, u32[]{:S(2)}, u32[]{:S(2)}) collective-permute-start(bf16[4,4,112,128]{3,2,1,0:T(8,128)(2,1)S(1)} %pad_maximum_fusion.2.rest_2_), channel_id=1, source_target_pairs={{0,8},{1,9},{2,10},{3,11},{4,12},{5,13},{6,14},{7,15},{8,16},{9,17... | collective-permute-start | bytes 1376264 | tf_op jit(solution)/shard_map/ppermute | solution.py:565
  179.3 16.2 %collective-permute-start.16 = (bf16[4,4,112,128]{3,2,1,0:T(8,128)(2,1)S(1)}, bf16[4,4,112,128]{3,2,1,0:T(8,128)(2,1)S(1)}, u32[]{:S(2)}, u32[]{:S(2)}) collective-permute-start(bf16[4,4,112,128]{3,2,1,0:T(8,128)(2,1)S(1)} %pad_maximum_fusion.3.rest_3_), channel_id=1, source_target_pairs={{0,24},{1,25},{2,26},{3,27},{4,28},{5,29},{6,30},{7,31},{8,0},{9,1... | collective-permute-start | bytes 1376264 | tf_op jit(solution)/shard_map/ppermute | solution.py:565
  191.8 3.9 %collective-permute-start.8 = (bf16[64,48,128]{2,1,0:T(8,128)(2,1)S(1)}, bf16[64,48,128]{2,1,0:T(8,128)(2,1)S(1)}, u32[]{:S(2)}, u32[]{:S(2)}) collective-permute-start(bf16[64,48,128]{2,1,0:T(8,128)(2,1)S(1)} %get-tuple-element.57), channel_id=1, source_target_pairs={{0,1},{1,0},{2,3},{3,2},{4,5},{5,4},{6,7},{7,6},{8,9},{9,8},{10,11... | collective-permute-start | bytes 2359304 | tf_op jit(solution)/shard_map/ppermute | solution.py:565
  195.9 7.8 %collective-permute-start.11 = (bf16[4,4,48,128]{3,2,1,0:T(8,128)(2,1)S(1)}, bf16[4,4,48,128]{3,2,1,0:T(8,128)(2,1)S(1)}, u32[]{:S(2)}, u32[]{:S(2)}) collective-permute-start(bf16[4,4,48,128]{3,2,1,0:T(8,128)(2,1)S(1)} %bitcast.108), channel_id=1, source_target_pairs={{0,6},{1,7},{2,0},{3,1},{4,2},{5,3},{6,4},{7,5},{8,14},{9,15},{10,... | collective-permute-start | bytes 589832 | tf_op jit(solution)/shard_map/ppermute | solution.py:565
  196.3 9.3 %collective-permute-start.9 = (bf16[4,4,48,128]{3,2,1,0:T(8,128)(2,1)S(1)}, bf16[4,4,48,128]{3,2,1,0:T(8,128)(2,1)S(1)}, u32[]{:S(2)}, u32[]{:S(2)}) collective-permute-start(bf16[4,4,48,128]{3,2,1,0:T(8,128)(2,1)S(1)} %bitcast.107), channel_id=1, source_target_pairs={{0,4},{1,5},{2,6},{3,7},{4,0},{5,1},{6,2},{7,3},{8,12},{9,13},{10,... | collective-permute-start | bytes 589832 | tf_op jit(solution)/shard_map/ppermute | solution.py:565
  197.2 12.6 %collective-permute-start.10 = (bf16[4,4,48,128]{3,2,1,0:T(8,128)(2,1)S(1)}, bf16[4,4,48,128]{3,2,1,0:T(8,128)(2,1)S(1)}, u32[]{:S(2)}, u32[]{:S(2)}) collective-permute-start(bf16[4,4,48,128]{3,2,1,0:T(8,128)(2,1)S(1)} %bitcast.106), channel_id=1, source_target_pairs={{0,2},{1,3},{2,4},{3,5},{4,6},{5,7},{6,0},{7,1},{8,10},{9,11},{10,... | collective-permute-start | bytes 589832 | tf_op jit(solution)/shard_map/ppermute | solution.py:565
  198.1 14.2 %collective-permute-start.17 = (bf16[4,112,128]{2,1,0:T(8,128)(2,1)S(1)}, bf16[4,112,128]{2,1,0:T(8,128)(2,1)S(1)}, u32[]{:S(2)}, u32[]{:S(2)}) collective-permute-start(bf16[4,112,128]{2,1,0:T(8,128)(2,1)S(1)} %get-tuple-element.72), channel_id=1, source_target_pairs={{0,4},{1,5},{2,6},{3,7},{4,0},{5,1},{6,2},{7,3},{8,12},{9,13},{10,... | collective-permute-start | bytes 344072 | tf_op jit(solution)/shard_map/ppermute | solution.py:565
  202.3 10.2 %collective-permute-start.19 = (bf16[4,112,128]{2,1,0:T(8,128)(2,1)S(1)}, bf16[4,112,128]{2,1,0:T(8,128)(2,1)S(1)}, u32[]{:S(2)}, u32[]{:S(2)}) collective-permute-start(bf16[4,112,128]{2,1,0:T(8,128)(2,1)S(1)} %get-tuple-element.73), channel_id=1, source_target_pairs={{0,6},{1,7},{2,0},{3,1},{4,2},{5,3},{6,4},{7,5},{8,14},{9,15},{10,... | collective-permute-start | bytes 344072 | tf_op jit(solution)/shard_map/ppermute | solution.py:565
  203.7 10.3 %collective-permute-start.18 = (bf16[4,112,128]{2,1,0:T(8,128)(2,1)S(1)}, bf16[4,112,128]{2,1,0:T(8,128)(2,1)S(1)}, u32[]{:S(2)}, u32[]{:S(2)}) collective-permute-start(bf16[4,112,128]{2,1,0:T(8,128)(2,1)S(1)} %get-tuple-element.74), channel_id=1, source_target_pairs={{0,2},{1,3},{2,4},{3,5},{4,6},{5,7},{6,0},{7,1},{8,10},{9,11},{10,... | collective-permute-start | bytes 344072 | tf_op jit(solution)/shard_map/ppermute | solution.py:565
  210.0 8.3 %collective-permute-start.12 = (bf16[4,144,128]{2,1,0:T(8,128)(2,1)S(1)}, bf16[4,144,128]{2,1,0:T(8,128)(2,1)S(1)}, u32[]{:S(2)}, u32[]{:S(2)}) collective-permute-start(bf16[4,144,128]{2,1,0:T(8,128)(2,1)S(1)} %get-tuple-element.69), channel_id=1, source_target_pairs={{0,16},{1,17},{2,18},{3,19},{4,20},{5,21},{6,22},{7,23},{8,24},{9,... | collective-permute-start | bytes 442376 | tf_op jit(solution)/shard_map/ppermute | solution.py:565
  210.1 8.2 %collective-permute-start.14 = (bf16[4,144,128]{2,1,0:T(8,128)(2,1)S(1)}, bf16[4,144,128]{2,1,0:T(8,128)(2,1)S(1)}, u32[]{:S(2)}, u32[]{:S(2)}) collective-permute-start(bf16[4,144,128]{2,1,0:T(8,128)(2,1)S(1)} %get-tuple-element.70), channel_id=1, source_target_pairs={{0,24},{1,25},{2,26},{3,27},{4,28},{5,29},{6,30},{7,31},{8,0},{9,1... | collective-permute-start | bytes 442376 | tf_op jit(solution)/shard_map/ppermute | solution.py:565
  212.3 8.1 %collective-permute-start.13 = (bf16[4,144,128]{2,1,0:T(8,128)(2,1)S(1)}, bf16[4,144,128]{2,1,0:T(8,128)(2,1)S(1)}, u32[]{:S(2)}, u32[]{:S(2)}) collective-permute-start(bf16[4,144,128]{2,1,0:T(8,128)(2,1)S(1)} %get-tuple-element.71), channel_id=1, source_target_pairs={{0,8},{1,9},{2,10},{3,11},{4,12},{5,13},{6,14},{7,15},{8,16},{9,17... | collective-permute-start | bytes 442376 | tf_op jit(solution)/shard_map/ppermute | solution.py:565
  220.5 6.5 %collective-permute-start.20 = (bf16[256,128]{1,0:T(8,128)(2,1)S(1)}, bf16[256,128]{1,0:T(8,128)(2,1)S(1)}, u32[]{:S(2)}, u32[]{:S(2)}) collective-permute-start(bf16[256,128]{1,0:T(8,128)(2,1)S(1)} %get-tuple-element.79), channel_id=1, source_target_pairs={{0,64},{1,65},{2,66},{3,67},{4,68},{5,69},{6,70},{7,71},{8,72},{9,... | collective-permute-start | bytes 196616 | tf_op jit(solution)/shard_map/ppermute | solution.py:565
  222.8 4.3 %collective-permute-start.22 = (bf16[256,128]{1,0:T(8,128)(2,1)S(1)}, bf16[256,128]{1,0:T(8,128)(2,1)S(1)}, u32[]{:S(2)}, u32[]{:S(2)}) collective-permute-start(bf16[256,128]{1,0:T(8,128)(2,1)S(1)} %get-tuple-element.80), channel_id=1, source_target_pairs={{0,96},{1,97},{2,98},{3,99},{4,100},{5,101},{6,102},{7,103},{8,104... | collective-permute-start | bytes 196616 | tf_op jit(solution)/shard_map/ppermute | solution.py:565
  223.9 5.5 %collective-permute-start.21 = (bf16[256,128]{1,0:T(8,128)(2,1)S(1)}, bf16[256,128]{1,0:T(8,128)(2,1)S(1)}, u32[]{:S(2)}, u32[]{:S(2)}) collective-permute-start(bf16[256,128]{1,0:T(8,128)(2,1)S(1)} %get-tuple-element.81), channel_id=1, source_target_pairs={{0,32},{1,33},{2,34},{3,35},{4,36},{5,37},{6,38},{7,39},{8,40},{9,... | collective-permute-start | bytes 196616 | tf_op jit(solution)/shard_map/ppermute | solution.py:565
Sparse Core Ops, SparseCore 0:
  11.6 83.8 all-gather.2
